TPU v7x, 32 devices: a whole 2x2x4 slice. The times are simulated.
32 devices in a mesh: batch: 8 (over z, core), exp: 4 (over y, x).
Axes of the slice: x: 2, y: 2, z: 4, core: 2. Of those that a mesh axis runs over, the one named last changes fastest.
Arguments:
- layer_input: bfloat16 [32, 1024, 512], P(('batch', 'exp')), may hold values from -6 to 6
- memory: bfloat16 [32, 1024, 512], P(('batch', 'exp')), may hold values from -6 to 6
- routes: int32 [32, 8, 1], P(('batch', 'exp')), may hold values from 0 to 3; in each aligned block of 8 rows (0 to 7, 8 to 15, ..., all dimensions but the last counted through in order) at most 4 rows name the same one
- out_grad: bfloat16 [32, 1024, 512], P(('batch', 'exp')), may hold values from -6 to 6
- self_gain: float32 [512], replicated, may hold values from 0.25 to 1.75
- self_shift: float32 [512], replicated, may hold values from -3 to 3
- self_project: bfloat16 [512, 1536], replicated, may hold values from -0.375 to 0.375
- self_output: bfloat16 [512, 512], replicated, may hold values from -1.5 to 1.5
- cross_gain: float32 [512], replicated, may hold values from 0.25 to 1.75
- cross_shift: float32 [512], replicated, may hold values from -3 to 3
- cross_query: bfloat16 [512, 512], replicated, may hold values from -0.375 to 0.375
- cross_memory: bfloat16 [512, 1024], replicated, may hold values from -0.375 to 0.375
- cross_output: bfloat16 [512, 512], replicated, may hold values from -0.75 to 0.75
- moe_gain: float32 [512], replicated, may hold values from 0.25 to 1.75
- moe_shift: float32 [512], replicated, may hold values from -3 to 3
- expert_up: bfloat16 [4, 512, 2048], P('exp'), may hold values from -0.25 to 0.25
- up_bias: float32 [4, 2048], P('exp'), may hold values from -3 to 3
- expert_down: bfloat16 [4, 2048, 512], P('exp'), may hold values from -0.125 to 0.125
- down_bias: float32 [4, 512], P('exp'), may hold values from -2 to 2
Outputs:
- layer_output: bfloat16 [32, 1024, 512], P(('batch', 'exp'))
- grad_input: float32 [32, 1024, 512], P(('batch', 'exp'))
- grad_memory: float32 [32, 1024, 512], P(('batch', 'exp'))
- grad_self_gain: float32 [512], replicated
- grad_self_shift: float32 [512], replicated
- grad_self_project: float32 [512, 1536], replicated
- grad_self_output: float32 [512, 512], replicated
- grad_cross_gain: float32 [512], replicated
- grad_cross_shift: float32 [512], replicated
- grad_cross_query: float32 [512, 512], replicated
- grad_cross_memory: float32 [512, 1024], replicated
- grad_cross_output: float32 [512, 512], replicated
- grad_moe_gain: float32 [512], replicated
- grad_moe_shift: float32 [512], replicated
- grad_expert_up: float32 [4, 512, 2048], P('exp', 'batch')
- grad_up_bias: float32 [4, 2048], P('exp', 'batch')
- grad_expert_down: float32 [4, 2048, 512], P('exp', 'batch')
- grad_down_bias: float32 [4, 512], P('exp', 'batch')
Inputs may be any that keep to these rules, and one draw needn't show every extreme that they name: `routes`: the 128 tokens of a group all go to the expert that the group's entry names; the 8 entries of one sequence name no expert more than 4 times.
All inputs are finite; a program needn't handle non-finite values.
Results may differ from a plain program's by a relative error of at most 0.02.
The roundings to bfloat16 on the way count: a program that leaves them out, or rounds other values in their place, can miss the bound.
Values may be sent and summed in bfloat16 or wider, within the bound.
A program may use at most 192 MiB of HBM per device.

v0:
```python
import jax
import jax.numpy as jnp
from jax import lax
from jax.sharding import PartitionSpec as P

HEADS = 8
HEAD_DIM = 64
CAPACITY = 4


EPSILON = 1e-05
NEGATIVE = -1e30


def layer_norm(values, gain, shift):
    center = values - jnp.mean(values, -1, keepdims=True)
    return center * lax.rsqrt(jnp.mean(center * center, -1, keepdims=True) + EPSILON) * gain + shift


def split_heads(values):
    return values.reshape(values.shape[0], HEADS, HEAD_DIM)


def merge_heads(values):
    return values.reshape(values.shape[0], HEADS * HEAD_DIM)


def contract(left, right, left_dim, right_dim):
    return lax.dot_general(
        left, right, (((left_dim,), (right_dim,)), ((), ())), preferred_element_type=jnp.float32
    )


def masked_scores(query, keys, query_place, key_place, causal):
    scores = jnp.einsum(
        "qhd,khd->hqk", query, keys, preferred_element_type=jnp.float32
    ) * HEAD_DIM ** (-0.5)
    if causal:
        scores = jnp.where((query_place[:, None] >= key_place[None, :])[None], scores, NEGATIVE)
    return scores


def attend(query, keys, values, causal):
    length = query.shape[0]
    block = min(512, length)
    count = length // block
    key_place = jnp.arange(keys.shape[0], dtype=jnp.int32)

    def forward_block(operands):
        piece, start = operands
        scores = masked_scores(
            piece, keys, start + jnp.arange(block, dtype=jnp.int32), key_place, causal
        )
        highest = jnp.max(scores, -1, keepdims=True)
        weights = jnp.exp(scores - highest)
        totals = jnp.sum(weights, -1, keepdims=True)
        probs = (weights / totals).astype(jnp.bfloat16)
        result = jnp.einsum("hqk,khd->qhd", probs, values, preferred_element_type=jnp.float32)
        return (merge_heads(result), (highest + jnp.log(totals))[:, :, 0])

    starts = jnp.arange(count, dtype=jnp.int32) * block
    result, log_total = lax.map(
        forward_block, (query.reshape(count, block, HEADS, HEAD_DIM), starts)
    )
    return (result.reshape(length, HEADS * HEAD_DIM), log_total)


def attend_back(query, keys, values, grad_out, log_total, causal):
    length = query.shape[0]
    block = min(512, length)
    count = length // block
    scale = HEAD_DIM ** (-0.5)
    key_place = jnp.arange(keys.shape[0], dtype=jnp.int32)

    def back_block(carry, operands):
        grad_keys, grad_values = carry
        piece, grad_piece, totals, start = operands
        scores = masked_scores(
            piece, keys, start + jnp.arange(block, dtype=jnp.int32), key_place, causal
        )
        probs = jnp.exp(scores - totals[:, :, None])
        grad_probs = jnp.einsum(
            "qhd,khd->hqk", grad_piece, values, preferred_element_type=jnp.float32
        )
        row_dot = jnp.sum(probs * grad_probs, -1, keepdims=True)
        grad_scores = (probs * (grad_probs - row_dot)).astype(jnp.bfloat16)
        grad_query = (
            jnp.einsum("hqk,khd->qhd", grad_scores, keys, preferred_element_type=jnp.float32)
            * scale
        )
        grad_keys = (
            grad_keys
            + jnp.einsum("hqk,qhd->khd", grad_scores, piece, preferred_element_type=jnp.float32)
            * scale
        )
        grad_values = grad_values + jnp.einsum(
            "hqk,qhd->khd",
            probs.astype(jnp.bfloat16),
            grad_piece,
            preferred_element_type=jnp.float32,
        )
        return ((grad_keys, grad_values), grad_query)

    zeros = jnp.zeros(keys.shape, jnp.float32)
    starts = jnp.arange(count, dtype=jnp.int32) * block
    (grad_keys, grad_values), grad_query = lax.scan(
        back_block,
        (zeros, zeros),
        (
            query.reshape(count, block, HEADS, HEAD_DIM),
            grad_out.reshape(count, block, HEADS, HEAD_DIM),
            log_total,
            starts,
        ),
    )
    return (grad_query.reshape(length, HEADS, HEAD_DIM), grad_keys, grad_values)


def placement(route, slots):
    groups = route.shape[0]
    same = route[:, None] == route[None, :]
    earlier = (
        jnp.arange(groups, dtype=jnp.int32)[None, :] < jnp.arange(groups, dtype=jnp.int32)[:, None]
    )
    rank = jnp.sum(jnp.logical_and(same, earlier), 1)
    slot = route * CAPACITY + rank
    return (slot[None, :] == jnp.arange(slots, dtype=jnp.int32)[:, None]).astype(jnp.bfloat16)


def expert_pre(flat, up_weight, up_shift):
    return jnp.dot(flat, up_weight, preferred_element_type=jnp.float32) + up_shift


def expert_back(pre, grad_flat, up_weight, down_weight):
    hidden, gelu_back = jax.vjp(jax.nn.gelu, pre)
    grad_pre = gelu_back(contract(grad_flat, down_weight, 1, 1))[0].astype(jnp.bfloat16)
    grad_rows = contract(grad_pre, up_weight, 1, 1).astype(jnp.bfloat16)
    return (hidden.astype(jnp.bfloat16), grad_pre, grad_rows)


def body(
    layer_input,
    memory,
    routes,
    out_grad,
    self_gain,
    self_shift,
    self_project,
    self_output,
    cross_gain,
    cross_shift,
    cross_query,
    cross_memory,
    cross_output,
    moe_gain,
    moe_shift,
    expert_up,
    up_bias,
    expert_down,
    down_bias,
):
    inputs = layer_input[0].astype(jnp.float32)
    rows = inputs.shape[0]
    width = inputs.shape[1]
    size = lax.axis_size("exp")
    up_weight = expert_up[0]
    down_weight = expert_down[0]
    up_shift = up_bias[0]
    down_shift = down_bias[0]
    normed1, norm1_back = jax.vjp(layer_norm, inputs, self_gain, self_shift)
    normed1_low = normed1.astype(jnp.bfloat16)
    project = jnp.dot(normed1_low, self_project, preferred_element_type=jnp.float32).astype(
        jnp.bfloat16
    )
    query = split_heads(project[:, :width])
    keys = split_heads(project[:, width : 2 * width])
    values = split_heads(project[:, 2 * width :])
    attn_out, self_total = attend(query, keys, values, True)
    attn_low = attn_out.astype(jnp.bfloat16)
    hidden1 = inputs + jnp.dot(attn_low, self_output, preferred_element_type=jnp.float32)
    normed2, norm2_back = jax.vjp(layer_norm, hidden1, cross_gain, cross_shift)
    normed2_low = normed2.astype(jnp.bfloat16)
    cross_q = jnp.dot(normed2_low, cross_query, preferred_element_type=jnp.float32).astype(
        jnp.bfloat16
    )
    memory_kv = jnp.dot(memory[0], cross_memory, preferred_element_type=jnp.float32).astype(
        jnp.bfloat16
    )
    memory_keys = split_heads(memory_kv[:, :width])
    memory_values = split_heads(memory_kv[:, width:])
    cross_out, cross_total = attend(split_heads(cross_q), memory_keys, memory_values, False)
    cross_low = cross_out.astype(jnp.bfloat16)
    hidden2 = hidden1 + jnp.dot(cross_low, cross_output, preferred_element_type=jnp.float32)
    normed3, norm3_back = jax.vjp(layer_norm, hidden2, moe_gain, moe_shift)
    normed3_low = normed3.astype(jnp.bfloat16)
    route = routes[0, :, 0]
    groups = route.shape[0]
    group_rows = rows // groups
    slots = size * CAPACITY
    place = placement(route, slots)
    send = jnp.einsum(
        "sg,grd->srd",
        place,
        normed3_low.reshape(groups, group_rows, width),
        preferred_element_type=jnp.float32,
    ).astype(jnp.bfloat16)
    send = send.reshape(size, CAPACITY * group_rows, width)
    send_grad = jnp.einsum(
        "sg,grd->srd",
        place,
        out_grad[0].reshape(groups, group_rows, width),
        preferred_element_type=jnp.float32,
    ).astype(jnp.bfloat16)
    send_grad = send_grad.reshape(send.shape)
    received = lax.all_to_all(send, "exp", split_axis=0, concat_axis=0, tiled=True)
    pre = expert_pre(received.reshape(-1, width), up_weight, up_shift)
    hidden = jax.nn.gelu(pre).astype(jnp.bfloat16)
    rows_out = (
        jnp.dot(hidden, down_weight, preferred_element_type=jnp.float32) + down_shift
    ).astype(jnp.bfloat16)
    returned = lax.all_to_all(
        rows_out.reshape(received.shape), "exp", split_axis=0, concat_axis=0, tiled=True
    )
    returned, received, pre_kept = (
        returned,
        received,
        pre.reshape(received.shape[0], received.shape[1], -1),
    )
    received_grad = lax.all_to_all(send_grad, "exp", split_axis=0, concat_axis=0, tiled=True)
    hidden_low, grad_pre, grad_rows = expert_back(
        pre_kept.reshape(-1, pre_kept.shape[-1]),
        received_grad.reshape(-1, width),
        up_weight,
        down_weight,
    )
    returned_grad = lax.all_to_all(
        grad_rows.reshape(received.shape), "exp", split_axis=0, concat_axis=0, tiled=True
    )
    expert_rows = jnp.einsum(
        "sg,srd->grd",
        place,
        returned.reshape(slots, group_rows, width),
        preferred_element_type=jnp.float32,
    ).reshape(rows, width)
    layer_output = (hidden2 + expert_rows).astype(jnp.bfloat16)
    flat = received.reshape(-1, width)
    grad_flat = received_grad.reshape(-1, width)
    grad_down = contract(hidden_low, grad_flat, 0, 0)
    grad_down_shift = jnp.sum(grad_flat.astype(jnp.float32), 0)
    grad_up = contract(flat, grad_pre, 0, 0)
    grad_up_shift = jnp.sum(grad_pre.astype(jnp.float32), 0)
    expert_sums = (
        lax.psum_scatter(
            grad_up.astype(jnp.bfloat16), "batch", scatter_dimension=0, tiled=True
        ).astype(jnp.float32),
        lax.psum_scatter(
            grad_up_shift.astype(jnp.bfloat16), "batch", scatter_dimension=0, tiled=True
        ).astype(jnp.float32),
        lax.psum_scatter(
            grad_down.astype(jnp.bfloat16), "batch", scatter_dimension=0, tiled=True
        ).astype(jnp.float32),
        lax.psum_scatter(
            grad_down_shift.astype(jnp.bfloat16), "batch", scatter_dimension=0, tiled=True
        ).astype(jnp.float32),
    )
    grad3 = out_grad[0].astype(jnp.float32)
    grad_normed3 = jnp.einsum(
        "sg,srd->grd",
        place,
        returned_grad.reshape(slots, group_rows, width),
        preferred_element_type=jnp.float32,
    ).reshape(rows, width)
    grad_h2_part, grad_moe_gain, grad_moe_shift = norm3_back(grad_normed3)
    grad2 = grad3 + grad_h2_part
    grad2_low = grad2.astype(jnp.bfloat16)
    grad_cross_output = contract(cross_low, grad2_low, 0, 0)
    grad_cross = contract(grad2_low, cross_output, 1, 1).astype(jnp.bfloat16)
    grad_cq, grad_ck, grad_cv = attend_back(
        split_heads(cross_q),
        memory_keys,
        memory_values,
        split_heads(grad_cross),
        cross_total,
        False,
    )
    grad_memory_kv = jnp.concatenate([merge_heads(grad_ck), merge_heads(grad_cv)], 1).astype(
        jnp.bfloat16
    )
    grad_cross_memory = contract(memory[0], grad_memory_kv, 0, 0)
    grad_memory = contract(grad_memory_kv, cross_memory, 1, 1)
    grad_cq_low = merge_heads(grad_cq).astype(jnp.bfloat16)
    grad_cross_query = contract(normed2_low, grad_cq_low, 0, 0)
    grad_normed2 = contract(grad_cq_low, cross_query, 1, 1)
    grad_h1_part, grad_cross_gain, grad_cross_shift = norm2_back(grad_normed2)
    grad1 = grad2 + grad_h1_part
    grad1_low = grad1.astype(jnp.bfloat16)
    grad_self_output = contract(attn_low, grad1_low, 0, 0)
    grad_attn = contract(grad1_low, self_output, 1, 1).astype(jnp.bfloat16)
    grad_query, grad_keys, grad_values = attend_back(
        query, keys, values, split_heads(grad_attn), self_total, True
    )
    grad_project = jnp.concatenate(
        [merge_heads(grad_query), merge_heads(grad_keys), merge_heads(grad_values)], 1
    ).astype(jnp.bfloat16)
    grad_self_project = contract(normed1_low, grad_project, 0, 0)
    grad_normed1 = contract(grad_project, self_project, 1, 1)
    grad_x_part, grad_self_gain, grad_self_shift = norm1_back(grad_normed1)
    grad_input = grad1 + grad_x_part
    shared = lax.psum(
        (
            grad_self_gain,
            grad_self_shift,
            grad_self_project,
            grad_self_output,
            grad_cross_gain,
            grad_cross_shift,
            grad_cross_query,
            grad_cross_memory,
            grad_cross_output,
            grad_moe_gain,
            grad_moe_shift,
        ),
        ("batch", "exp"),
    )
    return (
        layer_output[None],
        grad_input[None],
        grad_memory[None],
        shared[0],
        shared[1],
        shared[2],
        shared[3],
        shared[4],
        shared[5],
        shared[6],
        shared[7],
        shared[8],
        shared[9],
        shared[10],
        expert_sums[0][None],
        expert_sums[1][None],
        expert_sums[2][None],
        expert_sums[3][None],
    )


def solution(mesh):
    return jax.shard_map(
        body,
        mesh=mesh,
        in_specs=(
            P(("batch", "exp"), None, None),
            P(("batch", "exp"), None, None),
            P(("batch", "exp"), None, None),
            P(("batch", "exp"), None, None),
            P(),
            P(),
            P(),
            P(),
            P(),
            P(),
            P(),
            P(),
            P(),
            P(),
            P(),
            P("exp", None, None),
            P("exp", None),
            P("exp", None, None),
            P("exp", None),
        ),
        out_specs=(
            P(("batch", "exp"), None, None),
            P(("batch", "exp"), None, None),
            P(("batch", "exp"), None, None),
            P(),
            P(),
            P(),
            P(),
            P(),
            P(),
            P(),
            P(),
            P(),
            P(),
            P(),
            P("exp", "batch", None),
            P("exp", "batch"),
            P("exp", "batch", None),
            P("exp", "batch"),
        ),
        check_vma=False,
    )
```

profile of v0, /device:TPU:0, one launch (start us, length us, event | category | flops | bytes accessed | tf_op | source)
XLA Modules:
  0.0 682.0 jit_solution(17559410607470074538)
XLA Ops:
  32.4 39.7 %while.56 = (s32[]{:T(128)}, bf16[2,512,512]{2,1,0:T(8,128)(2,1)}, f32[2,8,512]{2,1,0:T(8,128)S(1)}, s32[2]{0:T(128)S(1)}, bf16[2,512,8,64]{1,3,2,0:T(8,128)(2,1...) while((s32[]{:T(128)}, bf16[2,512,512]{2,1,0:T(8,128)(2,1)}, ...), condition=%wide.region_5.6_spmd.clone, body=%wide.region_2.5_spmd.clone.sunk | while | flops 1124594176 | bytes 62001300 | solution.py:62
  42.7 5.8 fusion.216
  62.4 5.8 fusion.216
  85.6 32.3 %while.55 = (s32[]{:T(128)}, bf16[2,512,512]{2,1,0:T(8,128)(2,1)}, f32[2,8,512]{2,1,0:T(8,128)S(1)}, bf16[2,512,8,64]{1,3,2,0:T(8,128)(2,1)}, bf16[1024,8,64]{0,...) while((s32[]{:T(128)}, bf16[2,512,512]{2,1,0:T(8,128)(2,1)}, f32[2,8,512]{2,1,0:T(8,128)S(1)}, ...), condition=%wide.region_11.12_spmd, body=%wide.region_8.11_spmd.sunk | while | flops 1111486464 | bytes 59900028 | solution.py:62
  125.5 5.2 all-to-all-start
  135.3 21.1 %all-to-all-done = bf16[4,512,512]{2,1,0:T(8,128)(2,1)} async-done(((bf16[4,512,512]{2,1,0:T(8,128)(2,1)}), bf16[4,512,512]{2,1,0:T(8,128)(2,1)}, u32[]{:S(2)}, u32[]{:S(2)}) %all-to-all-start) | async-done | bytes 2097184 | tf_op jit(solution)/shard_map/all_to_all | solution.py:215
  161.0 14.6 %multiply_convert_fusion.2 = (bf16[2048,2048]{1,0:T(8,128)(2,1)}, f32[2048,2048]{1,0:T(8,128)}) fusion(f32[2048]{0:T(1024)S(1)} %bitcast.354, bf16[2048,512]{1,0:T(8,128)(2,1)} %bitcast.16, bf16[1,512,2048]{2,1,0:T(8,128)(2,1)S(1)} %copy-done), kind=kOutput, calls=%fused_computation.93 | convolution fusion | flops 4336910336 | bytes 29368320 | tf_op jit(solution)/shard_map/dot_general | solution.py:131
  175.6 10.0 %all-to-all-done.2 = bf16[4,512,512]{2,1,0:T(8,128)(2,1)} async-done(((bf16[4,512,512]{2,1,0:T(8,128)(2,1)}), bf16[4,512,512]{2,1,0:T(8,128)(2,1)}, u32[]{:S(2)}, u32[]{:S(2)}) %all-to-all-start.2) | async-done | bytes 2097184 | tf_op jit(solution)/shard_map/all_to_all | solution.py:229
  185.6 9.9 %convolution_convert_fusion.1 = bf16[2048,512]{1,0:T(8,128)(2,1)} fusion(bf16[2048,2048]{1,0:T(8,128)(2,1)} %get-tuple-element.601, bf16[2048,512]{1,0:T(8,128)(2,1)} %bitcast.28), kind=kOutput, calls=%fused_computation.100 | convolution fusion | flops 4296015872 | bytes 12582912 | tf_op jit(solution)/shard_map/dot_general | solution.py:29
  196.2 9.8 %add_convert_fusion = bf16[2048,512]{1,0:T(8,128)(2,1)} fusion(bf16[2048,2048]{1,0:T(8,128)(2,1)} %get-tuple-element.601, bf16[1,2048,512]{2,1,0:T(8,128)(2,1)} %param.44, f32[512]{0:T(512)S(1)} %bitcast.356), kind=kOutput, calls=%fused_computation.94 | convolution fusion | flops 4297064448 | bytes 12584960 | tf_op jit(solution)/shard_map/dot_general | solution.py:219
  210.7 18.6 %fusion.132 = (bf16[2048]{0:T(1024)(128)(2,1)}, bf16[2048,2048]{1,0:T(8,128)(2,1)S(1)}) fusion(f32[2048,2048]{1,0:T(8,128)} %get-tuple-element.602, f32[2048]{0:T(1024)S(1)} %bitcast.355, bf16[2048,512]{1,0:T(8,128)(2,1)} %bitcast.28, bf16[1,2048,512]{2,1,0:T(8,128)(2,1)} %param.44), kind=kOutput, calls=%fused_computation.205 | convolution fusion | flops 4387239936 | bytes 29372416 | tf_op jit(solution)/shard_map/dot_general | solution.py:29
  232.6 6.1 convolution_convert_fusion.3
  242.9 9.9 %convolution_convert_fusion.2 = bf16[512,2048]{1,0:T(8,128)(2,1)} fusion(bf16[2048,512]{1,0:T(8,128)(2,1)} %bitcast.16, bf16[2048,2048]{1,0:T(8,128)(2,1)} %copy-done.93), kind=kOutput, calls=%fused_computation.101 | convolution fusion | flops 4296015872 | bytes 12582912 | tf_op jit(solution)/shard_map/dot_general | solution.py:29
  258.6 8.0 %all-to-all-done.3 = bf16[4,512,512]{2,1,0:T(8,128)(2,1)S(1)} async-done(((bf16[4,512,512]{2,1,0:T(8,128)(2,1)}), bf16[4,512,512]{2,1,0:T(8,128)(2,1)S(1)}, u32[]{:S(2)}, u32[]{:S(2)}) %all-to-all-start.3) | async-done | bytes 2097184 | tf_op jit(solution)/shard_map/all_to_all | solution.py:236
  283.6 75.5 %while.57 = (s32[]{:T(128)}, f32[1024,8,64]{0,2,1:T(8,128)}, f32[1024,8,64]{0,2,1:T(8,128)}, bf16[2,512,8,64]{1,3,2,0:T(8,128)(2,1)}, bf16[2,512,8,64]{1,3,2,0:T...) while((s32[]{:T(128)}, f32[1024,8,64]{0,2,1:T(8,128)}, ...), condition=%wide.region_19.20_spmd.clone, body=%wide.region_17.19_spmd.clone.sunk | while | flops 2737565696 | bytes 195150096 | solution.py:106
  290.6 9.6 %multiply_reduce_fusion.12 = (f32[8,512]{1,0:T(8,128)S(1)}, f32[8,512,1024]{2,1,0:T(8,128)}) fusion(f32[8,512,1024]{2,1,0:T(8,128)S(1)} %fusion.226, f32[8,512]{1,0:T(8,128)S(1)} %dynamic-slice_bitcast_fusion.4, bf16[1024,8,64]{0,2,1:T(8,128)(2,1)} %get-tuple-element.896, bf16[2,512,8,64]{1,3,2,0:T(8,128)(2,1)} %get-tuple-element.895, s32[]{:T(128)S(6)} %copy.201), kind=kOutput, calls=%fused_computation.31.clone.1 | convolution fusion | flops 553644032 | bytes 35160068 | tf_op jit(solution)/shard_map/while/body/eval_jaxpr/qhd,khd->hqk/dot_general | solution.py:82
  300.3 10.4 %multiply_convert_fusion.5 = bf16[8,512,1024]{2,1,0:T(8,128)(2,1)} fusion(f32[8,512,1024]{2,1,0:T(8,128)} %get-tuple-element.807, f32[8,512,1024]{2,1,0:T(8,128)S(1)} %fusion.226, f32[8,512]{1,0:T(8,128)S(1)} %get-tuple-element.808, f32[8,512]{1,0:T(8,128)S(1)} %dynamic-slice_bitcast_fusion.4), kind=kLoop, calls=%fused_computation.30.clone.1 | loop fusion | flops 20971520 | bytes 41975808 | tf_op jit(solution)/shard_map/while/body/eval_jaxpr/convert_element_type | solution.py:86
  310.6 7.0 %fusion.227 = bf16[2,512,8,64]{1,3,2,0:T(8,128)(2,1)} fusion(bf16[2,512,8,64]{1,3,2,0:T(8,128)(2,1)} %get-tuple-element.880, s32[]{:T(128)S(6)} %copy.201, bf16[8,512,1024]{2,1,0:T(8,128)(2,1)} %multiply_convert_fusion.5, bf16[1024,8,64]{0,2,1:T(8,128)(2,1)S(1)} %get-tuple-element.893), kind=kOutput, calls=%fused_computation.41.clone.1 | convolution fusion | flops 537133056 | bytes 10485764 | tf_op jit(solution)/shard_map/while/body/eval_jaxpr/hqk,khd->qhd/dot_general | solution.py:88
  323.2 5.6 bitcast_add_fusion.10
  328.8 9.6 %multiply_reduce_fusion.12 = (f32[8,512]{1,0:T(8,128)S(1)}, f32[8,512,1024]{2,1,0:T(8,128)}) fusion(f32[8,512,1024]{2,1,0:T(8,128)S(1)} %fusion.226, f32[8,512]{1,0:T(8,128)S(1)} %dynamic-slice_bitcast_fusion.4, bf16[1024,8,64]{0,2,1:T(8,128)(2,1)} %get-tuple-element.896, bf16[2,512,8,64]{1,3,2,0:T(8,128)(2,1)} %get-tuple-element.895, s32[]{:T(128)S(6)} %copy.201), kind=kOutput, calls=%fused_computation.31.clone.1 | convolution fusion | flops 553644032 | bytes 35160068 | tf_op jit(solution)/shard_map/while/body/eval_jaxpr/qhd,khd->hqk/dot_general | solution.py:82
  338.4 10.4 %multiply_convert_fusion.5 = bf16[8,512,1024]{2,1,0:T(8,128)(2,1)} fusion(f32[8,512,1024]{2,1,0:T(8,128)} %get-tuple-element.807, f32[8,512,1024]{2,1,0:T(8,128)S(1)} %fusion.226, f32[8,512]{1,0:T(8,128)S(1)} %get-tuple-element.808, f32[8,512]{1,0:T(8,128)S(1)} %dynamic-slice_bitcast_fusion.4), kind=kLoop, calls=%fused_computation.30.clone.1 | loop fusion | flops 20971520 | bytes 41975808 | tf_op jit(solution)/shard_map/while/body/eval_jaxpr/convert_element_type | solution.py:86
  348.8 7.0 %fusion.227 = bf16[2,512,8,64]{1,3,2,0:T(8,128)(2,1)} fusion(bf16[2,512,8,64]{1,3,2,0:T(8,128)(2,1)} %get-tuple-element.880, s32[]{:T(128)S(6)} %copy.201, bf16[8,512,1024]{2,1,0:T(8,128)(2,1)} %multiply_convert_fusion.5, bf16[1024,8,64]{0,2,1:T(8,128)(2,1)S(1)} %get-tuple-element.893), kind=kOutput, calls=%fused_computation.41.clone.1 | convolution fusion | flops 537133056 | bytes 10485764 | tf_op jit(solution)/shard_map/while/body/eval_jaxpr/hqk,khd->qhd/dot_general | solution.py:88
  372.8 89.0 %while.58 = (s32[]{:T(128)}, f32[1024,8,64]{0,2,1:T(8,128)}, f32[1024,8,64]{0,2,1:T(8,128)}, bf16[2,512,8,64]{1,3,2,0:T(8,128)(2,1)}, bf16[2,512,8,64]{1,3,2,0:T...) while((s32[]{:T(128)}, f32[1024,8,64]{0,2,1:T(8,128)}, ...), condition=%wide.region_24.25_spmd.clone, body=%wide.region_22.24_spmd.clone.sunk | while | flops 2725507584 | bytes 191975728 | solution.py:106
  380.5 11.5 %multiply_reduce_fusion.13 = (f32[8,512]{1,0:T(8,128)}, f32[8,512,1024]{2,1,0:T(8,128)}) fusion(f32[8,512,1024]{2,1,0:T(8,128)S(1)} %fusion.237, f32[8,512]{1,0:T(8,128)} %dynamic-slice_bitcast_fusion.5, bf16[1024,8,64]{0,2,1:T(8,128)(2,1)S(1)} %get-tuple-element.929, bf16[2,512,8,64]{1,3,2,0:T(8,128)(2,1)} %get-tuple-element.927, s32[]{:T(128)S(6)} %copy.213, ...), kind=kOutput, calls=%fused_computation.59.clone.1 | convolution fusion | flops 557838336 | bytes 35684356 | tf_op jit(solution)/shard_map/while/body/eval_jaxpr/qhd,khd->hqk/dot_general | solution.py:35
  392.0 9.4 %multiply_convert_fusion.6 = bf16[8,512,1024]{2,1,0:T(8,128)(2,1)} fusion(f32[8,512,1024]{2,1,0:T(8,128)} %get-tuple-element.819, f32[8,512,1024]{2,1,0:T(8,128)S(1)} %fusion.237, f32[8,512]{1,0:T(8,128)} %get-tuple-element.820), kind=kLoop, calls=%fused_computation.58.clone.1 | loop fusion | flops 12582912 | bytes 41959424 | tf_op jit(solution)/shard_map/while/body/eval_jaxpr/convert_element_type | solution.py:86
  401.4 8.8 %bitcast_add_fusion.12 = f32[1024,8,64]{0,2,1:T(8,128)} fusion(f32[1024,8,64]{0,2,1:T(8,128)} %get-tuple-element.913, f32[8,512,1024]{2,1,0:T(8,128)} %get-tuple-element.819, pred[]{:T(512)S(6)} %compare.7, bf16[2,512,8,64]{1,3,2,0:T(8,128)(2,1)S(1)} %copy-done.16, s32[]{:T(128)S(6)} %copy.213), kind=kOutput, calls=%fused_computation.63.clone.1 | convolution fusion | flops 542113792 | bytes 21495812 | tf_op jit(solution)/shard_map/while/body/eval_jaxpr/hqk,qhd->khd/dot_general | solution.py:96
  423.4 11.5 %multiply_reduce_fusion.13 = (f32[8,512]{1,0:T(8,128)}, f32[8,512,1024]{2,1,0:T(8,128)}) fusion(f32[8,512,1024]{2,1,0:T(8,128)S(1)} %fusion.237, f32[8,512]{1,0:T(8,128)} %dynamic-slice_bitcast_fusion.5, bf16[1024,8,64]{0,2,1:T(8,128)(2,1)S(1)} %get-tuple-element.929, bf16[2,512,8,64]{1,3,2,0:T(8,128)(2,1)} %get-tuple-element.927, s32[]{:T(128)S(6)} %copy.213, ...), kind=kOutput, calls=%fused_computation.59.clone.1 | convolution fusion | flops 557838336 | bytes 35684356 | tf_op jit(solution)/shard_map/while/body/eval_jaxpr/qhd,khd->hqk/dot_general | solution.py:35
  434.9 9.4 %multiply_convert_fusion.6 = bf16[8,512,1024]{2,1,0:T(8,128)(2,1)} fusion(f32[8,512,1024]{2,1,0:T(8,128)} %get-tuple-element.819, f32[8,512,1024]{2,1,0:T(8,128)S(1)} %fusion.237, f32[8,512]{1,0:T(8,128)} %get-tuple-element.820), kind=kLoop, calls=%fused_computation.58.clone.1 | loop fusion | flops 12582912 | bytes 41959424 | tf_op jit(solution)/shard_map/while/body/eval_jaxpr/convert_element_type | solution.py:86
  444.3 9.4 %bitcast_add_fusion.12 = f32[1024,8,64]{0,2,1:T(8,128)} fusion(f32[1024,8,64]{0,2,1:T(8,128)} %get-tuple-element.913, f32[8,512,1024]{2,1,0:T(8,128)} %get-tuple-element.819, pred[]{:T(512)S(6)} %compare.7, bf16[2,512,8,64]{1,3,2,0:T(8,128)(2,1)S(1)} %copy-done.16, s32[]{:T(128)S(6)} %copy.213), kind=kOutput, calls=%fused_computation.63.clone.1 | convolution fusion | flops 542113792 | bytes 21495812 | tf_op jit(solution)/shard_map/while/body/eval_jaxpr/hqk,qhd->khd/dot_general | solution.py:96
  488.7 17.0 %all-reduce.4 = (bf16[2048]{0:T(1024)(128)(2,1)S(1)}, bf16[512]{0:T(512)(128)(2,1)S(1)}) all-reduce(bf16[2048]{0:T(1024)(128)(2,1)S(1)} %copy-done.75, bf16[512]{0:T(512)(128)(2,1)S(1)} %reduce_sum.299), channel_id=3, replica_groups=mesh['batch'=8,'exp'=4] {'batch'}, use_global_device_ids=true, to_apply=%region_46.47.clone | all-reduce | flops 2560 | bytes 10240
  514.0 38.6 %all-reduce.2 = (f32[512]{0:T(512)}, f32[512]{0:T(512)}, f32[512]{0:T(512)}, f32[512]{0:T(512)}, f32[512]{0:T(512)}, /*index=5*/f32[512]{0:T(512)}) all-reduce(f32[512]{0:T(512)S(1)} %get-tuple-element.497, f32[512]{0:T(512)S(1)} %get-tuple-element.500, f32[512]{0:T(512)S(1)} %copy-done.78, ...), channel_id=1, replica_groups=mesh['batch'=8,'exp'=4] {'batch','exp'}, use_global_device_ids=true, to_apply=%region_28.29 | all-reduce | flops 3072 | bytes 24576 | tf_op jit(solution)/shard_map/psum | solution.py:309
  562.9 102.9 %all-reduce.7.cloned.1.call-done = (f32[512,1536]{1,0:T(8,128)}, f32[512,512]{1,0:T(8,128)}, f32[512,512]{1,0:T(8,128)}, f32[512,1024]{0,1:T(8,128)}, f32[512,512]{1,0:T(8,128)}) async-done(((f32[512,1536]{1,0:T(8,128)}, f32[512,512]{1,0:T(8,128)}, f32[512,512]{1,0:T(8,128)}, f32[512,1024]{0,1:T(8,128)}, f32[512,512]{1,0:T(8,128)}), (f32[512,1536]{1,0:T(8,128)}, f32[512,512]{1,0:T(8,128)}, ...) | async-done | bytes 8388624 | tf_op jit(solution)/shard_map/psum | solution.py:309
  (363 shorter events, 258.9 us)
Async XLA Ops:
  8.0 153.0 %copy-start = (bf16[1,512,2048]{2,1,0:T(8,128)(2,1)S(1)}, bf16[1,512,2048]{2,1,0:T(8,128)(2,1)}, u32[]{:S(2)}) copy-start(bf16[1,512,2048]{2,1,0:T(8,128)(2,1)} %param.42) | copy-start | bytes 6291460
  8.0 6.0 copy-start.81
  8.1 6.0 copy-start.83
  11.8 5.2 copy-start.53
  81.1 4.5 copy-start.4
  125.5 30.9 %all-to-all-start = ((bf16[4,512,512]{2,1,0:T(8,128)(2,1)}), bf16[4,512,512]{2,1,0:T(8,128)(2,1)}, u32[]{:S(2)}, u32[]{:S(2)}) async-start(bf16[4,512,512]{2,1,0:T(8,128)(2,1)} %bitcast.332), calls=%async_computation | async-start | bytes 4194304 | tf_op jit(solution)/shard_map/all_to_all | solution.py:215
  156.4 4.6 copy-start.86
  156.4 29.2 %all-to-all-start.2 = ((bf16[4,512,512]{2,1,0:T(8,128)(2,1)}), bf16[4,512,512]{2,1,0:T(8,128)(2,1)}, u32[]{:S(2)}, u32[]{:S(2)}) async-start(bf16[4,512,512]{2,1,0:T(8,128)(2,1)} %bitcast.331), calls=%async_computation.2 | async-start | bytes 4194304 | tf_op jit(solution)/shard_map/all_to_all | solution.py:229
  161.0 398.4 %reduce-scatter.5.cloned.1.call-start = ((), (), s32[]{:S(2)}) async-start(), calls=%async_computation.7 | async-start | bytes 2359296 | tf_op jit(solution)/shard_map/reduce_scatter | solution.py:259
  206.0 32.7 %all-to-all-start.1 = ((bf16[4,512,512]{2,1,0:T(8,128)(2,1)}), bf16[4,512,512]{2,1,0:T(8,128)(2,1)}, u32[]{:S(2)}, u32[]{:S(2)}) async-start(bf16[4,512,512]{2,1,0:T(8,128)(2,1)} %bitcast.339), calls=%async_computation.1 | async-start | bytes 4194304 | tf_op jit(solution)/shard_map/all_to_all | solution.py:221
  238.7 28.0 %all-to-all-start.3 = ((bf16[4,512,512]{2,1,0:T(8,128)(2,1)}), bf16[4,512,512]{2,1,0:T(8,128)(2,1)S(1)}, u32[]{:S(2)}, u32[]{:S(2)}) async-start(bf16[4,512,512]{2,1,0:T(8,128)(2,1)} %bitcast.338), calls=%async_computation.3 | async-start | bytes 4194304 | tf_op jit(solution)/shard_map/all_to_all | solution.py:236
  242.9 318.3 %reduce-scatter.3.cloned.1.call-start = ((), (), s32[]{:S(2)}) async-start(), calls=%async_computation.6 | async-start | bytes 2359296 | tf_op jit(solution)/shard_map/reduce_scatter | solution.py:253
  252.8 413.0 %all-reduce.7.cloned.1.call-start = ((), (), s32[]{:S(2)}) async-start(), calls=%async_computation.8 | async-start | bytes 16777216 | tf_op jit(solution)/shard_map/psum | solution.py:309
  279.1 4.5 copy-start.11
  310.6 7.0 %copy-start.3 = (bf16[8,512,1024]{2,1,0:T(8,128)(2,1)S(1)}, bf16[8,512,1024]{2,1,0:T(8,128)(2,1)}, u32[]{:S(2)}) copy-start(bf16[8,512,1024]{2,1,0:T(8,128)(2,1)} %multiply_convert_fusion.5) | copy-start | bytes 25165828 | tf_op jit(solution)/shard_map/while
  310.6 7.0 %copy-start.7 = (f32[1024,8,64]{0,2,1:T(8,128)S(1)}, f32[1024,8,64]{0,2,1:T(8,128)}, u32[]{:S(2)}) copy-start(f32[1024,8,64]{0,2,1:T(8,128)} %get-tuple-element.878) | copy-start | bytes 6291460 | tf_op jit(solution)/shard_map/while
  348.8 7.0 %copy-start.3 = (bf16[8,512,1024]{2,1,0:T(8,128)(2,1)S(1)}, bf16[8,512,1024]{2,1,0:T(8,128)(2,1)}, u32[]{:S(2)}) copy-start(bf16[8,512,1024]{2,1,0:T(8,128)(2,1)} %multiply_convert_fusion.5) | copy-start | bytes 25165828 | tf_op jit(solution)/shard_map/while
  348.8 7.0 %copy-start.7 = (f32[1024,8,64]{0,2,1:T(8,128)S(1)}, f32[1024,8,64]{0,2,1:T(8,128)}, u32[]{:S(2)}) copy-start(f32[1024,8,64]{0,2,1:T(8,128)} %get-tuple-element.878) | copy-start | bytes 6291460 | tf_op jit(solution)/shard_map/while
  392.0 9.4 %copy-start.16 = (bf16[2,512,8,64]{1,3,2,0:T(8,128)(2,1)S(1)}, bf16[2,512,8,64]{1,3,2,0:T(8,128)(2,1)}, u32[]{:S(2)}) copy-start(bf16[2,512,8,64]{1,3,2,0:T(8,128)(2,1)} %get-tuple-element.931) | copy-start | bytes 3145732 | tf_op jit(solution)/shard_map/while
  401.4 8.8 %copy-start.2 = (bf16[8,512,1024]{2,1,0:T(8,128)(2,1)S(1)}, bf16[8,512,1024]{2,1,0:T(8,128)(2,1)}, u32[]{:S(2)}) copy-start(bf16[8,512,1024]{2,1,0:T(8,128)(2,1)} %multiply_convert_fusion.6) | copy-start | bytes 25165828 | tf_op jit(solution)/shard_map/while
  401.4 8.8 %copy-start.32 = (bf16[2,512,8,64]{1,3,2,0:T(8,128)(2,1)S(1)}, bf16[2,512,8,64]{1,3,2,0:T(8,128)(2,1)}, u32[]{:S(2)}) copy-start(bf16[2,512,8,64]{1,3,2,0:T(8,128)(2,1)} %get-tuple-element.914) | copy-start | bytes 3145732 | tf_op jit(solution)/shard_map/while
  434.9 9.4 %copy-start.16 = (bf16[2,512,8,64]{1,3,2,0:T(8,128)(2,1)S(1)}, bf16[2,512,8,64]{1,3,2,0:T(8,128)(2,1)}, u32[]{:S(2)}) copy-start(bf16[2,512,8,64]{1,3,2,0:T(8,128)(2,1)} %get-tuple-element.931) | copy-start | bytes 3145732 | tf_op jit(solution)/shard_map/while
  444.3 9.4 %copy-start.2 = (bf16[8,512,1024]{2,1,0:T(8,128)(2,1)S(1)}, bf16[8,512,1024]{2,1,0:T(8,128)(2,1)}, u32[]{:S(2)}) copy-start(bf16[8,512,1024]{2,1,0:T(8,128)(2,1)} %multiply_convert_fusion.6) | copy-start | bytes 25165828 | tf_op jit(solution)/shard_map/while
  444.3 9.4 %copy-start.32 = (bf16[2,512,8,64]{1,3,2,0:T(8,128)(2,1)S(1)}, bf16[2,512,8,64]{1,3,2,0:T(8,128)(2,1)}, u32[]{:S(2)}) copy-start(bf16[2,512,8,64]{1,3,2,0:T(8,128)(2,1)} %get-tuple-element.914) | copy-start | bytes 3145732 | tf_op jit(solution)/shard_map/while
  456.4 4.9 copy-start.33
  463.5 12.3 %copy-start.39 = (bf16[1024,8,64]{0,2,1:T(8,128)(2,1)}, bf16[1024,8,64]{0,2,1:T(8,128)(2,1)S(1)}, u32[]{:S(2)}) copy-start(bf16[1024,8,64]{0,2,1:T(8,128)(2,1)S(1)} %convert.30) | copy-start | bytes 3145732
  465.7 10.2 %copy-start.40 = (bf16[1024,8,64]{0,2,1:T(8,128)(2,1)}, bf16[1024,8,64]{0,2,1:T(8,128)(2,1)S(1)}, u32[]{:S(2)}) copy-start(bf16[1024,8,64]{0,2,1:T(8,128)(2,1)S(1)} %convert.31) | copy-start | bytes 3145732
  467.1 13.2 %copy-start.50 = (bf16[64,8,2,512]{3,1,2,0:T(8,128)(2,1)}, bf16[64,8,2,512]{3,1,2,0:T(8,128)(2,1)S(1)}, u32[]{:S(2)}) copy-start(bf16[64,8,2,512]{3,1,2,0:T(8,128)(2,1)S(1)} %copy.158) | copy-start | bytes 3145732
  469.2 11.1 %copy-start.41 = (bf16[1024,8,64]{0,2,1:T(8,128)(2,1)}, bf16[1024,8,64]{0,2,1:T(8,128)(2,1)S(1)}, u32[]{:S(2)}) copy-start(bf16[1024,8,64]{0,2,1:T(8,128)(2,1)S(1)} %convert.28) | copy-start | bytes 3145732
  471.8 8.5 %copy-start.42 = (bf16[1024,8,64]{0,2,1:T(8,128)(2,1)}, bf16[1024,8,64]{0,2,1:T(8,128)(2,1)S(1)}, u32[]{:S(2)}) copy-start(bf16[1024,8,64]{0,2,1:T(8,128)(2,1)S(1)} %convert.29) | copy-start | bytes 3145732
  506.9 4.6 copy-start.62
  552.6 4.7 copy-start.29
  (80 other events, 172.0 us)
Sparse Core Ops, SparseCore 0:
  195.7 36.0 reduce-scatter.4
  252.9 37.4 reduce-scatter.2
Sparse Core Ops, SparseCore 1:
  484.3 181.5 all-reduce.6
where the time goes:
time: 689 us; the launch traced here: 682 us
  matrix products  261 us (38%)
  waiting for transfers between devices  142 us (21%)
  local copies, waits for them, and re-layouts  93.2 us (14%)
  other arithmetic  90.9 us (13%)
  blocking collectives  55.7 us (8%)
  starting transfers between devices  19 us (3%)
  between operations  17.9 us (3%)
    psum x1, waiting for transfers between devices, body(): lax.psum((grad_self_gain, grad_self_shift, grad_self_project, grad_self_o...  103 us
    dot_general x14, matrix products, contract(): lax.dot_general(left, right, (((left_dim,), (right_dim,)), ((), ())), pre...  68.8 us
    dot_general x8, matrix products, masked_scores(): jnp.einsum('qhd,khd->hqk', query, keys, preferred_element_type=jnp.float32)  43 us
    convert_element_type x4, other arithmetic, back_block(): grad_scores = (probs * (grad_probs - row_dot)).astype(jnp.bfloat16)  39.5 us
    psum x1, blocking collectives, body(): lax.psum((grad_self_gain, grad_self_shift, grad_self_project, grad_self_o...  38.6 us
    unnamed x177, local copies, waits for them, and re-layouts  34.9 us
    dot_general x4, matrix products, back_block(): jnp.einsum('hqk,qhd->khd', probs.astype(jnp.bfloat16), grad_piece, prefer...  28.3 us
    dot_general x4, matrix products, back_block(): jnp.einsum('qhd,khd->hqk', grad_piece, values, preferred_element_type=jnp...  26.8 us
  transfers between devices with their start and end apart: 7, of which 4 were waited for; matrix products, arithmetic and copies ran while one was open for 43% of the time, Pallas kernels for 0%

commit v1 on v0

v1 whole, which is shorter than its diff:
```python
import functools
import math

import jax
import jax.numpy as jnp
from jax import lax
from jax.experimental import pallas as pl
from jax.experimental.pallas import tpu as pltpu
from jax.sharding import PartitionSpec as P

HEADS = 8
HEAD_DIM = 64
CAPACITY = 4
PAIR = 2 * HEAD_DIM
PAIRS = HEADS // 2
EPSILON = 1e-05
NEGATIVE = -1e30
SCALE = HEAD_DIM ** (-0.5)
SCALE2 = SCALE * math.log2(math.e)
BF = jnp.bfloat16
F32 = jnp.float32


def nn(left, right):
    return lax.dot_general(left, right, (((1,), (0,)), ((), ())), preferred_element_type=F32)


def nt(left, right):
    return lax.dot_general(left, right, (((1,), (1,)), ((), ())), preferred_element_type=F32)


def tn(left, right):
    return lax.dot_general(left, right, (((0,), (0,)), ((), ())), preferred_element_type=F32)


def span(index, size):
    return pl.ds(pl.multiple_of(index * size, size), size)


def normalize(values):
    center = values - jnp.mean(values, -1, keepdims=True)
    scale = lax.rsqrt(jnp.mean(center * center, -1, keepdims=True) + EPSILON)
    return center * scale, scale


def normalize_back(hat, scale, grad, gain):
    gained = grad * gain
    first = jnp.mean(gained, -1, keepdims=True)
    second = jnp.mean(gained * hat, -1, keepdims=True)
    return scale * (gained - first - hat * second)


def causal_mask(scores, block, causal):
    length = scores.shape[0]
    if not causal:
        return scores
    key = lax.broadcasted_iota(jnp.int32, (block, block), 0)
    row = lax.broadcasted_iota(jnp.int32, (block, block), 1)
    last = jnp.where(row >= key, scores[length - block :], NEGATIVE)
    if length == block:
        return last
    return jnp.concatenate([scores[: length - block], last], 0)


def own_head(values, head):
    lane = lax.broadcasted_iota(jnp.int32, values.shape, 1) < HEAD_DIM
    return jnp.where(lane if head == 0 else ~lane, values, jnp.zeros_like(values))


def attend(query, keys, values, out, out_t, total, causal, block=512):
    rows = out.shape[0]
    count = rows // block

    def pair(hp, _):
        def columns(column):
            return pl.ds(pl.multiple_of(column + hp * PAIR, PAIR), PAIR)

        two_keys = keys[0][:, columns(keys[1])]
        values_t = values[0][:, columns(values[1])].T
        results = {}

        def first(i, head):
            length = (i + 1) * block if causal else two_keys.shape[0]
            own = own_head(query[0][i * block : (i + 1) * block, columns(query[1])], head)
            return causal_mask(nt(two_keys[:length], own), block, causal)

        def second(i, head, scores):
            length = scores.shape[0]
            place = pl.ds(i * block, block)
            highest = jnp.max(scores, 0, keepdims=True)
            weights = jnp.exp2(scores * SCALE2 - highest * SCALE2).astype(BF)
            extended = jnp.concatenate(
                [
                    values_t[head * HEAD_DIM : (head + 1) * HEAD_DIM, :length],
                    jnp.ones((16, length), BF),
                ],
                0,
            )
            summed = nn(extended, weights)
            sums = summed[HEAD_DIM : HEAD_DIM + 1]
            total[hp, head : head + 1, place] = highest * SCALE2 + jnp.log2(sums)
            results[head] = summed[:HEAD_DIM] / sums
            if head == 1:
                both = jnp.concatenate([results[0], results[1]], 0).astype(BF)
                out_t[span(hp, PAIR), place] = both
                out[place, span(hp, PAIR)] = both.T

        before = None
        for i in range(count):
            for head in range(2):
                scores = first(i, head)
                if before is not None:
                    second(*before)
                before = (i, head, scores)
        second(*before)
        return 0

    lax.fori_loop(0, PAIRS, pair, 0)


def attend_back(
    query, keys, values, grad_out, out, total, grad_query, grad_keys, grad_values, sums, causal, block
):
    rows = grad_out.shape[0]
    count = rows // block

    def pair(hp, _):
        def columns(column):
            return pl.ds(pl.multiple_of(column + hp * PAIR, PAIR), PAIR)

        two_keys = keys[0][:, columns(keys[1])]
        two_values = values[0][:, columns(values[1])]
        keys_t = two_keys.T
        here = span(hp, PAIR)
        product = grad_out[:, here].astype(F32) * out[:, here].astype(F32)
        high = product.astype(BF)
        low = (product - high.astype(F32)).astype(BF)
        pick = (
            lax.broadcasted_iota(jnp.int32, (8, PAIR), 1) // HEAD_DIM
            == lax.broadcasted_iota(jnp.int32, (8, PAIR), 0)
        ).astype(F32).astype(BF)
        dots = nt(pick, high) + nt(pick, low)
        kept = {}

        def first(i, head):
            length = (i + 1) * block if causal else two_keys.shape[0]
            place = pl.ds(i * block, block)
            own_query = own_head(query[0][place, columns(query[1])], head)
            own_grad = own_head(grad_out[place, here], head)
            return (
                nt(two_keys[:length], own_query),
                nt(two_values[:length], own_grad),
                own_query,
                own_grad,
            )

        def second(i, head, state):
            scores, grad_probs, own_query, own_grad = state
            length = scores.shape[0]
            place = pl.ds(i * block, block)
            shifted = scores * SCALE2 - total[hp, head : head + 1, place]
            probs = jnp.exp2(causal_mask(shifted, block, causal))
            dot = dots[head : head + 1, i * block : (i + 1) * block]
            grad_scores = (probs * (grad_probs - dot)).astype(BF)
            back = nn(keys_t[head * HEAD_DIM : (head + 1) * HEAD_DIM, :length], grad_scores)
            kept[head] = (probs.astype(BF), grad_scores, own_query, own_grad, back)
            if head == 1:
                probs2, scores2 = [
                    jnp.concatenate([kept[0][n], kept[1][n]], 1) for n in range(2)
                ]
                query2, grad2 = [
                    jnp.concatenate([kept[0][n], kept[1][n]], 0) for n in range(2, 4)
                ]
                new_values = nn(probs2, grad2)
                new_keys = nn(scores2, query2)
                if i == count - 1:
                    sums[0][...] = new_keys
                    sums[1][...] = new_values
                else:
                    sums[0][:length] += new_keys
                    sums[1][:length] += new_values
                grad_query[0][place, columns(grad_query[1])] = (
                    jnp.concatenate([kept[0][4], kept[1][4]], 0).T * SCALE
                ).astype(BF)

        before = None
        for i in reversed(range(count)):
            for head in range(2):
                state = first(i, head)
                if before is not None:
                    second(*before)
                before = (i, head, state)
        second(*before)
        grad_keys[0][:, columns(grad_keys[1])] = (sums[0][...] * SCALE).astype(BF)
        grad_values[0][:, columns(grad_values[1])] = sums[1][...].astype(BF)
        return 0

    lax.fori_loop(0, PAIRS, pair, 0)


def slot_of(routes, group):
    own = routes[group]
    rank = lax.fori_loop(
        0, group, lambda j, c: c + jnp.where(routes[j] == own, 1, 0).astype(jnp.int32), jnp.int32(0)
    )
    return own * CAPACITY + rank


ROWS = 256


def front_kernel(
    group_rows,
    routes,
    x,
    memory,
    grad,
    self_gain,
    self_shift,
    self_project,
    self_output,
    cross_gain,
    cross_shift,
    cross_query,
    cross_memory,
    cross_output,
    moe_gain,
    moe_shift,
    project,
    attn,
    attn_t,
    total1,
    hidden1,
    cross_q,
    memory_kv,
    cross,
    cross_t,
    total2,
    hidden2,
    send,
    send_grad,
):
    rows, width = x.shape
    blocks = rows // ROWS
    send[...] = jnp.zeros_like(send)
    send_grad[...] = jnp.zeros_like(send_grad)

    def block1(i, _):
        here = span(i, ROWS)
        hat, _s = normalize(x[here].astype(F32))
        normed = (hat * self_gain[...] + self_shift[...]).astype(BF)
        project[here] = nn(normed, self_project[...]).astype(BF)
        memory_kv[here] = nn(memory[here], cross_memory[...]).astype(BF)
        return 0

    lax.fori_loop(0, blocks, block1, 0)
    attend((project, 0), (project, width), (project, 2 * width), attn, attn_t, total1, True)

    def block2(i, _):
        here = span(i, ROWS)
        hidden = x[here].astype(F32) + nn(attn[here], self_output[...])
        hidden1[here] = hidden
        hat, _s = normalize(hidden)
        normed = (hat * cross_gain[...] + cross_shift[...]).astype(BF)
        cross_q[here] = nn(normed, cross_query[...]).astype(BF)
        return 0

    lax.fori_loop(0, blocks, block2, 0)
    attend((cross_q, 0), (memory_kv, 0), (memory_kv, width), cross, cross_t, total2, False)

    def block3(i, _):
        here = span(i, ROWS)
        hidden = hidden1[here] + nn(cross[here], cross_output[...])
        hidden2[here] = hidden
        hat, _s = normalize(hidden)
        normed = (hat * moe_gain[...] + moe_shift[...]).astype(BF)
        for part in range(ROWS // group_rows):
            group = i * (ROWS // group_rows) + part
            slot = span(slot_of(routes, group), group_rows)
            send[slot] = normed[part * group_rows : (part + 1) * group_rows]
            send_grad[slot] = grad[span(group, group_rows)]
        return 0

    lax.fori_loop(0, blocks, block3, 0)


EXPERT_ROWS = 512


def experts_kernel(
    received,
    received_grad,
    up,
    up_bias,
    down,
    down_bias,
    rows_out,
    grad_rows,
    grad_up,
    grad_up_bias,
    grad_down,
    grad_down_bias,
    hidden,
    grad_pre,
    flat_t,
    grad_t,
):
    rows, width = received.shape
    wide = up.shape[1]
    chunk = 512
    first, third = math.sqrt(2.0 / math.pi), math.sqrt(2.0 / math.pi) * 0.044715
    flat_t[width:] = jnp.ones((flat_t.shape[0] - width, rows), BF)

    def block(i, _):
        here = span(i, EXPERT_ROWS)
        flat = received[here]
        grad = received_grad[here]
        flat_t[:width, here] = flat.T
        grad_t[:, here] = grad.T
        out = jnp.zeros((EXPERT_ROWS, width), F32)
        back = jnp.zeros((EXPERT_ROWS, width), F32)
        for c in range(wide // chunk):
            cols = pl.ds(c * chunk, chunk)
            pre = nn(flat, up[:, cols]) + up_bias[:, cols]
            square = pre * pre
            half = 0.5 + 0.5 * jnp.tanh(pre * (first + third * square))
            value = pre * half
            low = value.astype(BF)
            slope = half + value * (1.0 - half) * (2.0 * first + (6.0 * third) * square)
            gpre = (nt(grad, down[cols]) * slope).astype(BF)
            hidden[here, cols] = low
            grad_pre[here, cols] = gpre
            out += nn(low, down[cols])
            back += nt(gpre, up[:, cols])
        rows_out[here] = (out + down_bias[...]).astype(BF)
        grad_rows[here] = back.astype(BF)
        return 0

    lax.fori_loop(0, rows // EXPERT_ROWS, block, 0)

    def weights(c, _):
        cols = span(c, chunk)
        both = nn(flat_t[...], grad_pre[:, cols])
        grad_up[:, cols] = both[:width].astype(BF)
        grad_up_bias[:, cols] = both[width : width + 1].astype(BF)
        grad_down[cols] = nn(grad_t[...], hidden[:, cols]).T.astype(BF)
        return 0

    lax.fori_loop(0, wide // chunk, weights, 0)
    grad_down_bias[...] = jnp.sum(received_grad[...].astype(F32), 0, keepdims=True).astype(BF)


def back_kernel(
    group_rows,
    routes,
    x,
    memory,
    grad,
    self_gain,
    self_shift,
    self_project,
    self_output,
    cross_gain,
    cross_shift,
    cross_query,
    cross_memory,
    cross_output,
    moe_gain,
    moe_shift,
    project,
    attn,
    attn_t,
    total1,
    hidden1,
    cross_q,
    memory_kv,
    cross,
    cross_t,
    total2,
    hidden2,
    returned_grad,
    grad_input,
    grad_memory,
    grads,
    carried,
    carried_low,
    back_low,
    grad_q,
    grad_kv,
    grad_project,
    normed,
    sum_a,
    sum_b,
):
    rows, width = x.shape
    blocks = rows // ROWS
    zero = jnp.zeros((1, width), F32)
    per = ROWS // group_rows
    tail = grads.shape[0] - 16
    gains = []

    def block3(i, carry):
        here = span(i, ROWS)
        hat, scale = normalize(hidden2[here])
        gy = jnp.concatenate(
            [
                returned_grad[span(slot_of(routes, i * per + part), group_rows)]
                for part in range(per)
            ],
            0,
        ).astype(F32)
        total = grad[here].astype(F32) + normalize_back(hat, scale, gy, moe_gain[...])
        carried[here] = total
        low = total.astype(BF)
        carried_low[here] = low
        back_low[here] = nt(low, cross_output[...]).astype(BF)
        return (
            carry[0] + jnp.sum(gy * hat, 0, keepdims=True),
            carry[1] + jnp.sum(gy, 0, keepdims=True),
        )

    gains.append(lax.fori_loop(0, blocks, block3, (zero, zero)))
    grads[span(7, width)] = nn(cross_t[...], carried_low[...]).astype(BF)
    attend_back(
        (cross_q, 0),
        (memory_kv, 0),
        (memory_kv, width),
        back_low,
        cross,
        total2,
        (grad_q, 0),
        (grad_kv, 0),
        (grad_kv, width),
        (sum_a, sum_b),
        False,
        256,
    )

    def block2(i, carry):
        here = span(i, ROWS)
        hat, scale = normalize(hidden1[here])
        normed[here] = (hat * cross_gain[...] + cross_shift[...]).astype(BF)
        gy = nt(grad_q[here], cross_query[...])
        total = carried[here] + normalize_back(hat, scale, gy, cross_gain[...])
        carried[here] = total
        low = total.astype(BF)
        carried_low[here] = low
        back_low[here] = nt(low, self_output[...]).astype(BF)
        grad_memory[here] = nt(grad_kv[here], cross_memory[...])
        return (
            carry[0] + jnp.sum(gy * hat, 0, keepdims=True),
            carry[1] + jnp.sum(gy, 0, keepdims=True),
        )

    gains.append(lax.fori_loop(0, blocks, block2, (zero, zero)))
    grads[span(4, width)] = tn(normed[...], grad_q[...]).astype(BF)
    grads[span(5, width)] = tn(memory[...], grad_kv[:, :width]).astype(BF)
    grads[span(6, width)] = tn(memory[...], grad_kv[:, width:]).astype(BF)
    grads[span(3, width)] = nn(attn_t[...], carried_low[...]).astype(BF)
    attend_back(
        (project, 0),
        (project, width),
        (project, 2 * width),
        back_low,
        attn,
        total1,
        (grad_project, 0),
        (grad_project, width),
        (grad_project, 2 * width),
        (sum_a, sum_b),
        True,
        256,
    )

    def block1(i, carry):
        here = span(i, ROWS)
        hat, scale = normalize(x[here].astype(F32))
        normed[here] = (hat * self_gain[...] + self_shift[...]).astype(BF)
        gy = nt(grad_project[here], self_project[...])
        grad_input[here] = carried[here] + normalize_back(hat, scale, gy, self_gain[...])
        return (
            carry[0] + jnp.sum(gy * hat, 0, keepdims=True),
            carry[1] + jnp.sum(gy, 0, keepdims=True),
        )

    gains.append(lax.fori_loop(0, blocks, block1, (zero, zero)))
    for part in range(3):
        grads[span(part, width)] = tn(
            normed[...], grad_project[:, part * width : (part + 1) * width]
        ).astype(BF)
    small = [gains[2][0], gains[2][1], gains[1][0], gains[1][1], gains[0][0], gains[0][1]]
    grads[tail:] = jnp.concatenate(small + [jnp.zeros((10, width), F32)], 0).astype(BF)


def output_kernel(group_rows, routes, hidden2, returned, out):
    groups = out.shape[0] // group_rows

    def block(i, _):
        here = span(i, group_rows)
        moved = returned[span(slot_of(routes, i), group_rows)]
        out[here] = (hidden2[here] + moved.astype(F32)).astype(BF)
        return 0

    lax.fori_loop(0, groups, block, 0)


def call(kernel, inputs, outputs, scratch=(), scalars=0, flops=0):
    vmem = pl.BlockSpec(memory_space=pltpu.VMEM)
    smem = pl.BlockSpec(memory_space=pltpu.SMEM)
    return pl.pallas_call(
        kernel,
        out_shape=tuple(jax.ShapeDtypeStruct(shape, dtype) for shape, dtype in outputs),
        in_specs=[smem] * scalars + [vmem] * (len(inputs) - scalars),
        out_specs=tuple(vmem for _ in outputs),
        scratch_shapes=[pltpu.VMEM(shape, dtype) for shape, dtype in scratch],
        compiler_params=pltpu.CompilerParams(vmem_limit_bytes=60 << 20),
        cost_estimate=pl.CostEstimate(flops=flops, bytes_accessed=20 << 20, transcendentals=0),
    )(*inputs)


def body(
    layer_input,
    memory,
    routes,
    out_grad,
    self_gain,
    self_shift,
    self_project,
    self_output,
    cross_gain,
    cross_shift,
    cross_query,
    cross_memory,
    cross_output,
    moe_gain,
    moe_shift,
    expert_up,
    up_bias,
    expert_down,
    down_bias,
):
    x = layer_input[0]
    memory = memory[0]
    grad = out_grad[0]
    rows, width = x.shape
    wide = expert_up.shape[2]
    size = lax.axis_size("exp")
    groups = routes.shape[1]
    group_rows = rows // groups
    slot_rows = size * CAPACITY * group_rows
    route = routes.reshape(groups)
    gains = [v.reshape(1, width) for v in (self_gain, self_shift, cross_gain, cross_shift, moe_gain, moe_shift)]
    shared_in = [
        route, x, memory, grad,
        gains[0], gains[1], self_project, self_output,
        gains[2], gains[3], cross_query, cross_memory, cross_output,
        gains[4], gains[5],
    ]
    saved = call(
        functools.partial(front_kernel, group_rows),
        shared_in,
        [
            ((rows, 3 * width), BF),
            ((rows, width), BF),
            ((width, rows), BF),
            ((PAIRS, 8, rows), F32),
            ((rows, width), F32),
            ((rows, width), BF),
            ((memory.shape[0], 2 * width), BF),
            ((rows, width), BF),
            ((width, rows), BF),
            ((PAIRS, 8, rows), F32),
            ((rows, width), F32),
            ((slot_rows, width), BF),
            ((slot_rows, width), BF),
        ],
        scalars=1,
        flops=30 * 10**9,
    )
    send, send_grad = saved[-2:]
    saved = list(saved[:-2])
    hidden2 = saved[-1]

    def exchange(values):
        return lax.all_to_all(
            values.reshape(size, slot_rows // size, width), "exp", split_axis=0, concat_axis=0, tiled=True
        ).reshape(slot_rows, width)

    received_grad = exchange(send_grad)
    received = exchange(send)
    rows_out, grad_rows, grad_up, grad_up_bias, grad_down, grad_down_bias = call(
        experts_kernel,
        [received, received_grad, expert_up[0], up_bias, expert_down[0], down_bias],
        [
            ((slot_rows, width), BF),
            ((slot_rows, width), BF),
            ((width, wide), BF),
            ((1, wide), BF),
            ((wide, width), BF),
            ((1, width), BF),
        ],
        [
            ((slot_rows, wide), BF),
            ((slot_rows, wide), BF),
            ((width + 16, slot_rows), BF),
            ((width, slot_rows), BF),
        ],
        flops=26 * 10**9,
    )
    returned_grad = exchange(grad_rows)
    returned = exchange(rows_out)
    expert_sums = (
        lax.psum_scatter(grad_up, "batch", scatter_dimension=0, tiled=True).astype(F32),
        lax.psum_scatter(grad_up_bias, "batch", scatter_dimension=1, tiled=True).astype(F32),
        lax.psum_scatter(grad_down, "batch", scatter_dimension=0, tiled=True).astype(F32),
        lax.psum_scatter(grad_down_bias, "batch", scatter_dimension=1, tiled=True).astype(F32),
    )
    mats = 8
    grad_input, grad_memory, grads = call(
        functools.partial(back_kernel, group_rows),
        shared_in + saved + [returned_grad],
        [
            ((rows, width), F32),
            ((memory.shape[0], width), F32),
            ((mats * width + 16, width), BF),
        ],
        [
            ((rows, width), F32),
            ((rows, width), BF),
            ((rows, width), BF),
            ((rows, width), BF),
            ((memory.shape[0], 2 * width), BF),
            ((rows, 3 * width), BF),
            ((rows, width), BF),
            ((max(rows, memory.shape[0]), PAIR), F32),
            ((max(rows, memory.shape[0]), PAIR), F32),
        ],
        scalars=1,
        flops=60 * 10**9,
    )
    layer_output = call(
        functools.partial(output_kernel, group_rows),
        [route, hidden2, returned],
        [((rows, width), BF)],
        scalars=1,
        flops=10**6,
    )[0]
    grads = lax.psum(grads, ("batch", "exp")).astype(F32)
    mat = [grads[i * width : (i + 1) * width] for i in range(mats)]
    small = grads[mats * width :]
    return (
        layer_output[None],
        grad_input[None],
        grad_memory[None],
        small[0],
        small[1],
        jnp.concatenate(mat[0:3], 1),
        mat[3],
        small[2],
        small[3],
        mat[4],
        jnp.concatenate(mat[5:7], 1),
        mat[7],
        small[4],
        small[5],
        expert_sums[0][None],
        expert_sums[1],
        expert_sums[2][None],
        expert_sums[3],
    )


def solution(mesh):
    return jax.shard_map(
        body,
        mesh=mesh,
        in_specs=(
            P(("batch", "exp"), None, None),
            P(("batch", "exp"), None, None),
            P(("batch", "exp"), None, None),
            P(("batch", "exp"), None, None),
            P(),
            P(),
            P(),
            P(),
            P(),
            P(),
            P(),
            P(),
            P(),
            P(),
            P(),
            P("exp", None, None),
            P("exp", None),
            P("exp", None, None),
            P("exp", None),
        ),
        out_specs=(
            P(("batch", "exp"), None, None),
            P(("batch", "exp"), None, None),
            P(("batch", "exp"), None, None),
            P(),
            P(),
            P(),
            P(),
            P(),
            P(),
            P(),
            P(),
            P(),
            P(),
            P(),
            P("exp", "batch", None),
            P("exp", "batch"),
            P("exp", "batch", None),
            P("exp", "batch"),
        ),
        check_vma=False,
    )
```

time: 689 us -> 418 us (0.61)
  matrix products: 261 us -> 0 us
  Pallas kernels: 0 us -> 143 us
  other arithmetic: 90.9 us -> 8.02 us
  local copies, waits for them, and re-layouts: 93.2 us -> 12.1 us
  waiting for transfers between devices: 142 us -> 171 us
  starting transfers between devices: 19 us -> 7.8 us
    dot_general x53 -> x0, matrix products: 261 us -> none  [the longest x14 68.8 us: contract(): lax.dot_general(left, right, (((left_dim,), (right_dim,)), ((), ())), pre...]
    pallas_call x0 -> x4, Pallas kernels: none -> 143 us  [call(): pl.pallas_call(kernel, out_shape=tuple((jax.ShapeDtypeStruct(shape, dtype...]
    all_to_all x0 -> x2, blocking collectives: none -> 59.5 us  [exchange(): lax.all_to_all(values.reshape(size, slot_rows // size, width), 'exp', spl...]
    convert_element_type x7 -> x2, other arithmetic: 40.6 us -> 1.11 us  [the longest x1 0.59 us: body(): lax.psum_scatter(grad_up_bias, 'batch', scatter_dimension=1, tiled=True)]
    psum x1 -> x0, blocking collectives: 38.6 us -> none  [body(): lax.psum((grad_self_gain, grad_self_shift, grad_self_project, grad_self_o...]
    unnamed x177 -> x14, local copies, waits for them, and re-layouts: 34.9 us -> 6.26 us
    reduce_sum x14 -> x0, other arithmetic: 27.9 us -> none  [the longest x4 15.4 us: forward_block(): totals = jnp.sum(weights, -1, keepdims=True)]
    unnamed x1 -> x0, blocking collectives: 17 us -> none
  transfers between devices with their start and end apart: 7 -> 7, of which waited for: 4 -> 3; matrix products, arithmetic and copies ran while one was open for 43% -> 4% of each run, Pallas kernels for 0% -> 16%
where the time goes in v1:
time: 418 us; the launch traced here: 417 us
  waiting for transfers between devices  171 us (41%)
  Pallas kernels  143 us (34%)
  blocking collectives  59.5 us (14%)
  between operations  15.3 us (4%)
  local copies, waits for them, and re-layouts  12.1 us (3%)
  other arithmetic  8.02 us (2%)
  starting transfers between devices  7.8 us (2%)
    pallas_call x4, Pallas kernels, call(): pl.pallas_call(kernel, out_shape=tuple((jax.ShapeDtypeStruct(shape, dtype...  143 us
    psum x1, waiting for transfers between devices, body(): grads = lax.psum(grads, ('batch', 'exp')).astype(F32)  119 us
    all_to_all x2, blocking collectives, exchange(): lax.all_to_all(values.reshape(size, slot_rows // size, width), 'exp', spl...  59.5 us
    all_to_all x2, waiting for transfers between devices, exchange(): lax.all_to_all(values.reshape(size, slot_rows // size, width), 'exp', spl...  50.8 us
  transfers between devices with their start and end apart: 7, of which 3 were waited for; matrix products, arithmetic and copies ran while one was open for 4% of the time, Pallas kernels for 16%

profile of v1, /device:TPU:0, one launch (start us, length us, event | category | flops | bytes accessed | tf_op | source)
XLA Modules:
  0.0 417.4 jit_solution(8950120345815389096)
XLA Ops:
  8.0 40.7 %shard_map.322 = (bf16[1024,1536]{1,0:T(8,128)(2,1)}, bf16[1024,512]{1,0:T(8,128)(2,1)}, bf16[512,1024]{1,0:T(8,128)(2,1)}, f32[4,8,1024]{2,1,0:T(8,128)}, f32[1...) custom-call(s32[8]{0:T(128)} %bitcast.58, ...), custom_call_target="tpu_custom_call" | custom-call | flops 30000001024 | bytes 20971520 | tf_op jit(solution)/shard_map/pallas_call | solution.py:510
  48.7 31.5 %all_to_all.20 = bf16[4,512,512]{2,1,0:T(8,128)(2,1)} all-to-all(bf16[4,512,512]{2,1,0:T(8,128)(2,1)} %bitcast.44), channel_id=1, replica_groups=mesh['batch'=8,'exp'=4] {'exp'}, dimensions={0} | all-to-all | bytes 4194304 | tf_op jit(solution)/shard_map/all_to_all | solution.py:585
  80.2 28.0 %all_to_all.21 = bf16[4,512,512]{2,1,0:T(8,128)(2,1)} all-to-all(bf16[4,512,512]{2,1,0:T(8,128)(2,1)S(1)} %bitcast.43), channel_id=1, replica_groups=mesh['batch'=8,'exp'=4] {'exp'}, dimensions={0} | all-to-all | bytes 4194304 | tf_op jit(solution)/shard_map/all_to_all | solution.py:585
  108.2 36.6 %shard_map.323 = (bf16[2048,512]{1,0:T(8,128)(2,1)}, bf16[2048,512]{1,0:T(8,128)(2,1)}, bf16[512,2048]{1,0:T(8,128)(2,1)}, bf16[1,2048]{1,0:T(2,128)(2,1)}, bf16...) custom-call(bf16[2048,512]{1,0:T(8,128)(2,1)} %bitcast.46, bf16[2048,512]{1,0:T(8,128)(2,1)} %bitcast.45, ...), custom_call_target="tpu_custom_call" | custom-call | flops 25999998976 | bytes 20971520 | tf_op jit(solution)/shard_map/pallas_call | solution.py:510
  144.8 3.8 all-to-all-start.3
  148.6 0.0 reduce-scatter.15.cloned.1.call-start
  148.7 0.8 copy.39
  149.5 0.0 reduce-scatter.13.cloned.1.call-start
  149.6 1.1 copy.37
  150.6 0.3 all-reduce.2.cloned.1.call-start
  150.9 20.6 %all-to-all-done.3 = bf16[4,512,512]{2,1,0:T(8,128)(2,1)S(1)} async-done(((bf16[4,512,512]{2,1,0:T(8,128)(2,1)}), bf16[4,512,512]{2,1,0:T(8,128)(2,1)S(1)}, u32[]{:S(2)}, u32[]{:S(2)}) %all-to-all-start.3) | async-done | bytes 2097184 | tf_op jit(solution)/shard_map/all_to_all | solution.py:585
  171.5 1.3 copy-done.1
  172.9 62.4 %shard_map.325 = (f32[1024,512]{1,0:T(8,128)}, f32[1024,512]{1,0:T(8,128)}, bf16[4112,512]{1,0:T(8,128)(2,1)}) custom-call(s32[8]{0:T(128)} %bitcast.59, bf16[1024,512]{1,0:T(8,128)(2,1)} %bitcast.64, bf16[1024,512]{1,0:T(8,128)(2,1)} %bitcast.66, bf16[1024,512]{1,0:T(8,128)(2,1)} %bitcast.68, f32[1,512]{1,0:T(1,128)} %bitcast.70, f32[1,512]{1,0:T(1,128)} %bitcast.72, ...), custom_call_target="tpu_custom_call" | custom-call | flops 60000002048 | bytes 20971520 | tf_op jit(solution)/shard_map/pallas_call | solution.py:510
  235.3 0.0 reduce-scatter.11.cloned.1.call-start
  235.4 0.7 reduce-scatter.11.cloned.1.call-update
  236.1 0.0 reduce-scatter.9.cloned.1.call-start
  236.1 0.5 reduce-scatter.9.cloned.1.call-update
  236.6 3.6 all-to-all-start.2
  240.3 0.8 copy.40
  241.1 0.5 convert_element_type.13
  241.6 0.9 copy.38
  242.5 0.6 convert_element_type.12
  243.1 30.2 %all-to-all-done.2 = bf16[4,512,512]{2,1,0:T(8,128)(2,1)S(1)} async-done(((bf16[4,512,512]{2,1,0:T(8,128)(2,1)}), bf16[4,512,512]{2,1,0:T(8,128)(2,1)S(1)}, u32[]{:S(2)}, u32[]{:S(2)}) %all-to-all-start.2) | async-done | bytes 2097184 | tf_op jit(solution)/shard_map/all_to_all | solution.py:585
  273.3 1.3 copy-done
  274.6 3.7 shard_map.324
  278.3 119.3 %all-reduce.2.cloned.1.call-done = bf16[4112,512]{1,0:T(8,128)(2,1)} async-done(((bf16[4112,512]{1,0:T(8,128)(2,1)}), bf16[4112,512]{1,0:T(8,128)(2,1)}) %all-reduce.2.cloned.1.call-update) | async-done | bytes 4210704 | tf_op jit(solution)/shard_map/psum | solution.py:648
  397.6 4.3 %fusion.1 = (f32[512,512]{1,0:T(8,128)}, f32[512,512]{1,0:T(8,128)S(1)}, f32[512,512]{1,0:T(8,128)S(1)}, f32[512,512]{1,0:T(8,128)}, f32[512,512]{1,0:T(8,128)},...) fusion(bf16[4112,512]{1,0:T(8,128)(2,1)} %all-reduce.2.cloned.1.call-done), kind=kLoop, calls=%fused_computation.5 | loop fusion | bytes 16777216 | tf_op jit(solution)/shard_map/slice | solution.py:649
  401.9 1.5 pad_maximum_fusion.1
  403.3 1.5 fusion
  404.9 1.9 pad_maximum_fusion
  406.7 1.8 bitcast_convert_fusion
  408.5 1.8 bitcast_convert_fusion.1
  (15 shorter events, 0.1 us)
Async XLA Ops:
  48.7 31.5 %copy-start.2 = (bf16[2048,512]{1,0:T(8,128)(2,1)S(1)}, bf16[2048,512]{1,0:T(8,128)(2,1)}, u32[]{:S(2)}) copy-start(bf16[2048,512]{1,0:T(8,128)(2,1)} %get-tuple-element.41) | copy-start | bytes 6291460
  144.8 3.8 copy-start.4
  144.8 4.7 %copy-start.3 = (bf16[1,2048]{1,0:T(2,128)(2,1)S(1)}, bf16[1,2048]{1,0:T(2,128)(2,1)}, u32[]{:S(2)}) copy-start(bf16[1,2048]{1,0:T(2,128)(2,1)} %get-tuple-element.59) | copy-start | bytes 12292
  144.8 26.7 %all-to-all-start.3 = ((bf16[4,512,512]{2,1,0:T(8,128)(2,1)}), bf16[4,512,512]{2,1,0:T(8,128)(2,1)S(1)}, u32[]{:S(2)}, u32[]{:S(2)}) async-start(bf16[4,512,512]{2,1,0:T(8,128)(2,1)} %bitcast.42), calls=%async_computation.3 | async-start | bytes 4194304 | tf_op jit(solution)/shard_map/all_to_all | solution.py:585
  148.6 91.7 %reduce-scatter.15.cloned.1.call-start = ((), (), s32[]{:S(2)}) async-start(), calls=%async_computation.12 | async-start | bytes 147456
  149.5 92.1 %reduce-scatter.13.cloned.1.call-start = ((), (), s32[]{:S(2)}) async-start(), calls=%async_computation.11 | async-start | bytes 589824
  150.6 246.9 %all-reduce.2.cloned.1.call-start = ((), (), s32[]{:S(2)}) async-start(), calls=%async_computation.8 | async-start | bytes 8421376 | tf_op jit(solution)/shard_map/psum | solution.py:648
  171.5 1.3 copy-start.1
  235.3 171.4 %reduce-scatter.11.cloned.1.call-start = ((), (), s32[]{:S(2)}) async-start(), calls=%async_computation.10 | async-start | bytes 2359296 | tf_op jit(solution)/shard_map/reduce_scatter | solution.py:615
  236.1 172.5 %reduce-scatter.9.cloned.1.call-start = ((), (), s32[]{:S(2)}) async-start(), calls=%async_computation.9 | async-start | bytes 2359296 | tf_op jit(solution)/shard_map/reduce_scatter | solution.py:613
  236.6 36.7 %all-to-all-start.2 = ((bf16[4,512,512]{2,1,0:T(8,128)(2,1)}), bf16[4,512,512]{2,1,0:T(8,128)(2,1)S(1)}, u32[]{:S(2)}, u32[]{:S(2)}) async-start(bf16[4,512,512]{2,1,0:T(8,128)(2,1)} %bitcast.40), calls=%async_computation.2 | async-start | bytes 4194304 | tf_op jit(solution)/shard_map/all_to_all | solution.py:585
  273.3 1.3 copy-start
Sparse Core Ops, SparseCore 0:
  151.8 31.5 reduce-scatter.14
  186.1 29.1 reduce-scatter.12
  238.6 40.1 reduce-scatter.10
  281.0 41.8 reduce-scatter.8
Sparse Core Ops, SparseCore 1:
  235.4 162.1 all-reduce.1

commit v2 on v1

--- a/solution.py
+++ b/solution.py
@@ -102,7 +102,7 @@
             results[head] = summed[:HEAD_DIM] / sums
             if head == 1:
                 both = jnp.concatenate([results[0], results[1]], 0).astype(BF)
-                out_t[span(hp, PAIR), place] = both
+                out_t[pl.ds(pl.multiple_of(i * HEADS * HEAD_DIM + hp * PAIR, PAIR), PAIR)] = both
                 out[place, span(hp, PAIR)] = both.T
 
         before = None
@@ -198,18 +198,282 @@
     lax.fori_loop(0, PAIRS, pair, 0)
 
 
-def slot_of(routes, group):
+def slot_of(routes, group, device, size):
     own = routes[group]
     rank = lax.fori_loop(
         0, group, lambda j, c: c + jnp.where(routes[j] == own, 1, 0).astype(jnp.int32), jnp.int32(0)
     )
-    return own * CAPACITY + rank
+    return partner_of(device, own, size) * CAPACITY + rank
+
+
+def weigh(values, weight):
+    return values * jnp.full(values.shape, weight.astype(F32), F32).astype(BF)
+
+
+def pick_group(routes, source, group_rows, expert, rank):
+    count = jnp.int32(0)
+    total = None
+    for group in range(source.shape[0] // group_rows):
+        same = jnp.where(routes[group] == expert, 1, 0).astype(jnp.int32)
+        hit = same * jnp.where(count == rank, 1, 0).astype(jnp.int32)
+        count = count + same
+        term = weigh(source[group * group_rows : (group + 1) * group_rows], hit)
+        total = term if total is None else total + term
+    return total
+
+
+def partner_of(own, offset, size):
+    result, bit = 0, 1
+    while bit < size:
+        result = result + lax.rem(own // bit + offset // bit, 2) * bit
+        bit *= 2
+    return result
 
 
 ROWS = 256
-
-
-def front_kernel(
+MESH = pl.DeviceIdType.MESH
+Q, K, V, ATTN, CQ, MK, MV, CROSS, ATTN_T, CROSS_T = range(10)
+SAVED = 10
+
+
+def forward_kernel(
+    size,
+    group_rows,
+    routes,
+    self_gain,
+    self_shift,
+    cross_gain,
+    cross_shift,
+    moe_gain,
+    moe_shift,
+    up_bias,
+    down_bias,
+    *refs,
+):
+    (
+        x_h, memory_h, grad_h, project_h, output_h, query_h, memory_w_h, cross_w_h, up_h, down_h,
+        saved_o, hidden1_o, hidden2_o, rows_out_o, returned_o, grad_up_o, grad_down_o,
+        total1, total2, grad_up_bias, grad_down_bias,
+        x, memory, grad, self_project, self_output, cross_query, cross_memory, cross_output, up, down,
+        arena, hidden1, hidden2, normed3, outbound, received, received_grad, flat_t, grad_t, grad_up, grad_down,
+        in_sems, out_sems, grad_send, grad_recv, row_send, row_recv, back_send, back_recv,
+    ) = refs
+    rows, width = x.shape
+    wide = up.shape[1]
+    blocks = rows // ROWS
+    part_rows = CAPACITY * group_rows
+    slot_rows = size * part_rows
+    batch, own = lax.axis_index("batch"), lax.axis_index("exp")
+
+    def partner(offset):
+        return (batch, partner_of(own, offset, size))
+
+    loads = [
+        pltpu.make_async_copy(source, target, in_sems.at[n])
+        for n, (source, target) in enumerate(
+            [
+                (grad_h, grad), (x_h, x), (project_h, self_project), (memory_h, memory),
+                (memory_w_h, cross_memory), (output_h, self_output), (query_h, cross_query),
+                (cross_w_h, cross_output), (up_h, up), (down_h, down),
+            ]
+        )
+    ]
+    for load in loads:
+        load.start()
+    barrier = pltpu.get_barrier_semaphore()
+    for offset in range(1, size):
+        pl.semaphore_signal(barrier, inc=1, device_id=partner(offset), device_id_type=MESH)
+    pl.semaphore_wait(barrier, size - 1)
+
+    def part(ref, offset):
+        return ref.at[pl.ds(pl.multiple_of(offset * part_rows, part_rows), part_rows)]
+
+    def send(source, target, offset, send_sems, recv_sems):
+        return pltpu.make_async_remote_copy(
+            src_ref=part(source, offset),
+            dst_ref=part(target, offset),
+            send_sem=send_sems.at[offset],
+            recv_sem=recv_sems.at[offset],
+            device_id=partner(offset),
+            device_id_type=MESH,
+        )
+
+    def dispatch(source, target, offset):
+        expert = partner_of(own, offset, size)
+
+        def one(rank, _):
+            values = pick_group(routes, source, group_rows, expert, rank)
+            target[pl.ds(pl.multiple_of(offset * part_rows + rank * group_rows, group_rows), group_rows)] = values
+            return 0
+
+        lax.fori_loop(0, CAPACITY, one, 0)
+
+    def to_all(source, target, send_sems, recv_sems):
+        dispatch(source, target, 0)
+
+        def one(offset, _):
+            dispatch(source, outbound, offset)
+            send(outbound, target, offset, send_sems, recv_sems).start()
+            return 0
+
+        lax.fori_loop(1, size, one, 0)
+
+    loads[0].wait()
+    to_all(grad, received_grad, grad_send, grad_recv)
+    for load in loads[1:5]:
+        load.wait()
+
+    def place(which):
+        return arena.at[pl.ds(which * rows, rows)]
+
+    q, k, v, attn, cq, mk, mv, cross, attn_t, cross_t = [place(n) for n in range(SAVED)]
+
+    def block1(i, _):
+        here = span(i, ROWS)
+        hat, _s = normalize(x[here].astype(F32))
+        normed = (hat * self_gain[...] + self_shift[...]).astype(BF)
+        for n, target in enumerate((q, k, v)):
+            target[here] = nn(normed, self_project[:, n * width : (n + 1) * width]).astype(BF)
+        for n, target in enumerate((mk, mv)):
+            target[here] = nn(memory[here], cross_memory[:, n * width : (n + 1) * width]).astype(BF)
+        return 0
+
+    lax.fori_loop(0, blocks, block1, 0)
+    attend((q, 0), (k, 0), (v, 0), attn, attn_t, total1, True)
+    for load in loads[5:]:
+        load.wait()
+
+    def block2(i, _):
+        here = span(i, ROWS)
+        hidden = x[here].astype(F32) + nn(attn[here], self_output[...])
+        hidden1[here] = hidden
+        hat, _s = normalize(hidden)
+        normed = (hat * cross_gain[...] + cross_shift[...]).astype(BF)
+        cq[here] = nn(normed, cross_query[...]).astype(BF)
+        return 0
+
+    lax.fori_loop(0, blocks, block2, 0)
+    attend((cq, 0), (mk, 0), (mv, 0), cross, cross_t, total2, False)
+    stores = [
+        pltpu.make_async_copy(arena.at[pl.ds(0, SAVED * rows)], saved_o, out_sems.at[0]),
+        pltpu.make_async_copy(hidden1, hidden1_o, out_sems.at[1]),
+        pltpu.make_async_copy(hidden2, hidden2_o, out_sems.at[2]),
+    ]
+    stores[0].start()
+    stores[1].start()
+
+    def block3(i, _):
+        here = span(i, ROWS)
+        hidden = hidden1[here] + nn(cross[here], cross_output[...])
+        hidden2[here] = hidden
+        hat, _s = normalize(hidden)
+        normed3[here] = (hat * moe_gain[...] + moe_shift[...]).astype(BF)
+        return 0
+
+    lax.fori_loop(0, blocks, block3, 0)
+    stores[2].start()
+
+    def sent(source, target, send_sems, recv_sems):
+        def one(offset, _):
+            send(source, target, offset, send_sems, recv_sems).wait_send()
+            return 0
+
+        lax.fori_loop(1, size, one, 0)
+
+    sent(outbound, received_grad, grad_send, grad_recv)
+    to_all(normed3, received, row_send, row_recv)
+    stores[0].wait()
+
+    block_rows = max(512, part_rows)
+    per = block_rows // part_rows
+    chunk = 512
+    first, third = math.sqrt(2.0 / math.pi), math.sqrt(2.0 / math.pi) * 0.044715
+    flat_t[width:] = jnp.ones((flat_t.shape[0] - width, slot_rows), BF)
+
+    def hidden_at(c, start, length):
+        return arena.at[pl.ds(pl.multiple_of(c * slot_rows + start, block_rows), length)]
+
+    def pre_at(c, start, length):
+        return arena.at[
+            pl.ds(pl.multiple_of((wide // chunk + c) * slot_rows + start, block_rows), length)
+        ]
+
+    def block(i, bias):
+        for n in range(per):
+            offset = i * per + n
+
+            @pl.when(offset > 0)
+            def _():
+                send(outbound, received_grad, offset, grad_send, grad_recv).wait_recv()
+                send(outbound, received, offset, row_send, row_recv).wait_recv()
+
+        here = span(i, block_rows)
+        flat = received[here]
+        grads = received_grad[here]
+        flat_t[:width, here] = flat.T
+        grad_t[:, here] = grads.T
+        out = jnp.zeros((block_rows, width), F32)
+        back = jnp.zeros((block_rows, width), F32)
+        for c in range(wide // chunk):
+            cols = pl.ds(c * chunk, chunk)
+            pre = nn(flat, up[:, cols]) + up_bias[:, cols]
+            square = pre * pre
+            half = 0.5 + 0.5 * jnp.tanh(pre * (first + third * square))
+            value = pre * half
+            low = value.astype(BF)
+            slope = half + value * (1.0 - half) * (2.0 * first + (6.0 * third) * square)
+            gpre = (nt(grads, down[cols]) * slope).astype(BF)
+            hidden_at(c, i * block_rows, block_rows)[...] = low
+            pre_at(c, i * block_rows, block_rows)[...] = gpre
+            out += nn(low, down[cols])
+            back += nt(gpre, up[:, cols])
+        received[here] = (out + down_bias[...]).astype(BF)
+        received_grad[here] = back.astype(BF)
+        for n in range(per):
+            offset = i * per + n
+
+            @pl.when(offset > 0)
+            def _():
+                send(received_grad, returned_o, offset, back_send, back_recv).start()
+
+        return bias + jnp.sum(grads.astype(F32), 0, keepdims=True)
+
+    bias = lax.fori_loop(0, slot_rows // block_rows, block, jnp.zeros((1, width), F32))
+    grad_down_bias[...] = bias.astype(BF)
+    stores.append(
+        pltpu.make_async_copy(part(received_grad, 0), part(returned_o, 0), out_sems.at[3])
+    )
+    stores.append(pltpu.make_async_copy(received, rows_out_o, out_sems.at[4]))
+    stores[3].start()
+    stores[4].start()
+
+    def weights(c, _):
+        cols = span(c, chunk)
+        both = nn(flat_t[...], pre_at(c, 0, slot_rows)[...])
+        grad_up[:, cols] = both[:width].astype(BF)
+        grad_up_bias[:, cols] = both[width : width + 1].astype(BF)
+        grad_down[cols] = nn(grad_t[...], hidden_at(c, 0, slot_rows)[...]).T.astype(BF)
+        return 0
+
+    lax.fori_loop(0, wide // chunk, weights, 0)
+    stores.append(pltpu.make_async_copy(grad_up, grad_up_o, out_sems.at[5]))
+    stores.append(pltpu.make_async_copy(grad_down, grad_down_o, out_sems.at[6]))
+    stores[5].start()
+    stores[6].start()
+    sent(outbound, received, row_send, row_recv)
+    sent(received_grad, returned_o, back_send, back_recv)
+
+    def arrived(offset, _):
+        send(received_grad, returned_o, offset, back_send, back_recv).wait_recv()
+        return 0
+
+    lax.fori_loop(1, size, arrived, 0)
+    for store in stores[1:]:
+        store.wait()
+
+
+def back_kernel(
+    size,
     group_rows,
     routes,
     x,
@@ -226,156 +490,9 @@
     cross_output,
     moe_gain,
     moe_shift,
-    project,
-    attn,
-    attn_t,
+    saved,
     total1,
     hidden1,
-    cross_q,
-    memory_kv,
-    cross,
-    cross_t,
-    total2,
-    hidden2,
-    send,
-    send_grad,
-):
-    rows, width = x.shape
-    blocks = rows // ROWS
-    send[...] = jnp.zeros_like(send)
-    send_grad[...] = jnp.zeros_like(send_grad)
-
-    def block1(i, _):
-        here = span(i, ROWS)
-        hat, _s = normalize(x[here].astype(F32))
-        normed = (hat * self_gain[...] + self_shift[...]).astype(BF)
-        project[here] = nn(normed, self_project[...]).astype(BF)
-        memory_kv[here] = nn(memory[here], cross_memory[...]).astype(BF)
-        return 0
-
-    lax.fori_loop(0, blocks, block1, 0)
-    attend((project, 0), (project, width), (project, 2 * width), attn, attn_t, total1, True)
-
-    def block2(i, _):
-        here = span(i, ROWS)
-        hidden = x[here].astype(F32) + nn(attn[here], self_output[...])
-        hidden1[here] = hidden
-        hat, _s = normalize(hidden)
-        normed = (hat * cross_gain[...] + cross_shift[...]).astype(BF)
-        cross_q[here] = nn(normed, cross_query[...]).astype(BF)
-        return 0
-
-    lax.fori_loop(0, blocks, block2, 0)
-    attend((cross_q, 0), (memory_kv, 0), (memory_kv, width), cross, cross_t, total2, False)
-
-    def block3(i, _):
-        here = span(i, ROWS)
-        hidden = hidden1[here] + nn(cross[here], cross_output[...])
-        hidden2[here] = hidden
-        hat, _s = normalize(hidden)
-        normed = (hat * moe_gain[...] + moe_shift[...]).astype(BF)
-        for part in range(ROWS // group_rows):
-            group = i * (ROWS // group_rows) + part
-            slot = span(slot_of(routes, group), group_rows)
-            send[slot] = normed[part * group_rows : (part + 1) * group_rows]
-            send_grad[slot] = grad[span(group, group_rows)]
-        return 0
-
-    lax.fori_loop(0, blocks, block3, 0)
-
-
-EXPERT_ROWS = 512
-
-
-def experts_kernel(
-    received,
-    received_grad,
-    up,
-    up_bias,
-    down,
-    down_bias,
-    rows_out,
-    grad_rows,
-    grad_up,
-    grad_up_bias,
-    grad_down,
-    grad_down_bias,
-    hidden,
-    grad_pre,
-    flat_t,
-    grad_t,
-):
-    rows, width = received.shape
-    wide = up.shape[1]
-    chunk = 512
-    first, third = math.sqrt(2.0 / math.pi), math.sqrt(2.0 / math.pi) * 0.044715
-    flat_t[width:] = jnp.ones((flat_t.shape[0] - width, rows), BF)
-
-    def block(i, _):
-        here = span(i, EXPERT_ROWS)
-        flat = received[here]
-        grad = received_grad[here]
-        flat_t[:width, here] = flat.T
-        grad_t[:, here] = grad.T
-        out = jnp.zeros((EXPERT_ROWS, width), F32)
-        back = jnp.zeros((EXPERT_ROWS, width), F32)
-        for c in range(wide // chunk):
-            cols = pl.ds(c * chunk, chunk)
-            pre = nn(flat, up[:, cols]) + up_bias[:, cols]
-            square = pre * pre
-            half = 0.5 + 0.5 * jnp.tanh(pre * (first + third * square))
-            value = pre * half
-            low = value.astype(BF)
-            slope = half + value * (1.0 - half) * (2.0 * first + (6.0 * third) * square)
-            gpre = (nt(grad, down[cols]) * slope).astype(BF)
-            hidden[here, cols] = low
-            grad_pre[here, cols] = gpre
-            out += nn(low, down[cols])
-            back += nt(gpre, up[:, cols])
-        rows_out[here] = (out + down_bias[...]).astype(BF)
-        grad_rows[here] = back.astype(BF)
-        return 0
-
-    lax.fori_loop(0, rows // EXPERT_ROWS, block, 0)
-
-    def weights(c, _):
-        cols = span(c, chunk)
-        both = nn(flat_t[...], grad_pre[:, cols])
-        grad_up[:, cols] = both[:width].astype(BF)
-        grad_up_bias[:, cols] = both[width : width + 1].astype(BF)
-        grad_down[cols] = nn(grad_t[...], hidden[:, cols]).T.astype(BF)
-        return 0
-
-    lax.fori_loop(0, wide // chunk, weights, 0)
-    grad_down_bias[...] = jnp.sum(received_grad[...].astype(F32), 0, keepdims=True).astype(BF)
-
-
-def back_kernel(
-    group_rows,
-    routes,
-    x,
-    memory,
-    grad,
-    self_gain,
-    self_shift,
-    self_project,
-    self_output,
-    cross_gain,
-    cross_shift,
-    cross_query,
-    cross_memory,
-    cross_output,
-    moe_gain,
-    moe_shift,
-    project,
-    attn,
-    attn_t,
-    total1,
-    hidden1,
-    cross_q,
-    memory_kv,
-    cross,
-    cross_t,
     total2,
     hidden2,
     returned_grad,
@@ -398,13 +515,24 @@
     per = ROWS // group_rows
     tail = grads.shape[0] - 16
     gains = []
+    own = lax.axis_index("exp")
+    q, k, v, attn, cross_q, mk, mv, cross, attn_t, cross_t = [
+        saved.at[pl.ds(n * rows, rows)] for n in range(SAVED)
+    ]
+
+    def times(turned, right):
+        half = 512
+        return sum(
+            nn(turned[n * width : (n + 1) * width], right[n * half : (n + 1) * half])
+            for n in range(rows // half)
+        )
 
     def block3(i, carry):
         here = span(i, ROWS)
         hat, scale = normalize(hidden2[here])
         gy = jnp.concatenate(
             [
-                returned_grad[span(slot_of(routes, i * per + part), group_rows)]
+                returned_grad[span(slot_of(routes, i * per + part, own, size), group_rows)]
                 for part in range(per)
             ],
             0,
@@ -420,11 +548,11 @@
         )
 
     gains.append(lax.fori_loop(0, blocks, block3, (zero, zero)))
-    grads[span(7, width)] = nn(cross_t[...], carried_low[...]).astype(BF)
+    grads[span(7, width)] = times(cross_t, carried_low).astype(BF)
     attend_back(
         (cross_q, 0),
-        (memory_kv, 0),
-        (memory_kv, width),
+        (mk, 0),
+        (mv, 0),
         back_low,
         cross,
         total2,
@@ -456,11 +584,11 @@
     grads[span(4, width)] = tn(normed[...], grad_q[...]).astype(BF)
     grads[span(5, width)] = tn(memory[...], grad_kv[:, :width]).astype(BF)
     grads[span(6, width)] = tn(memory[...], grad_kv[:, width:]).astype(BF)
-    grads[span(3, width)] = nn(attn_t[...], carried_low[...]).astype(BF)
+    grads[span(3, width)] = times(attn_t, carried_low).astype(BF)
     attend_back(
-        (project, 0),
-        (project, width),
-        (project, 2 * width),
+        (q, 0),
+        (k, 0),
+        (v, 0),
         back_low,
         attn,
         total1,
@@ -492,12 +620,13 @@
     grads[tail:] = jnp.concatenate(small + [jnp.zeros((10, width), F32)], 0).astype(BF)
 
 
-def output_kernel(group_rows, routes, hidden2, returned, out):
+def output_kernel(size, group_rows, routes, hidden2, returned, out):
+    own = lax.axis_index("exp")
     groups = out.shape[0] // group_rows
 
     def block(i, _):
         here = span(i, group_rows)
-        moved = returned[span(slot_of(routes, i), group_rows)]
+        moved = returned[span(slot_of(routes, i, own, size), group_rows)]
         out[here] = (hidden2[here] + moved.astype(F32)).astype(BF)
         return 0
 
@@ -550,65 +679,69 @@
     slot_rows = size * CAPACITY * group_rows
     route = routes.reshape(groups)
     gains = [v.reshape(1, width) for v in (self_gain, self_shift, cross_gain, cross_shift, moe_gain, moe_shift)]
+    def array(shape, dtype):
+        return jax.ShapeDtypeStruct(shape, dtype)
+
+    vmem, smem, any_ = [pl.BlockSpec(memory_space=m) for m in (pltpu.VMEM, pltpu.SMEM, pl.ANY)]
+    big = [
+        x, memory, grad, self_project, self_output, cross_query, cross_memory, cross_output,
+        expert_up[0], expert_down[0],
+    ]
+    sems = pltpu.SemaphoreType.DMA((size,))
+    saved, hidden1, hidden2, rows_out, returned_grad, grad_up, grad_down, total1, total2, grad_up_bias, grad_down_bias = pl.pallas_call(
+        functools.partial(forward_kernel, size, group_rows),
+        out_shape=(
+            array((SAVED * rows, width), BF),
+            array((rows, width), F32),
+            array((rows, width), F32),
+            array((slot_rows, width), BF),
+            array((slot_rows, width), BF),
+            array((width, wide), BF),
+            array((wide, width), BF),
+            array((PAIRS, 8, rows), F32),
+            array((PAIRS, 8, rows), F32),
+            array((1, wide), BF),
+            array((1, width), BF),
+        ),
+        in_specs=[smem] + [vmem] * 8 + [any_] * 10,
+        out_specs=(any_,) * 7 + (vmem,) * 4,
+        scratch_shapes=[pltpu.VMEM(v.shape, v.dtype) for v in big]
+        + [
+            pltpu.VMEM(shape, dtype)
+            for shape, dtype in [
+                ((2 * slot_rows * (wide // 512), 512), BF),
+                ((rows, width), F32),
+                ((rows, width), F32),
+                ((rows, width), BF),
+                ((slot_rows, width), BF),
+                ((slot_rows, width), BF),
+                ((slot_rows, width), BF),
+                ((width + 16, slot_rows), BF),
+                ((width, slot_rows), BF),
+                ((width, wide), BF),
+                ((wide, width), BF),
+            ]
+        ]
+        + [pltpu.SemaphoreType.DMA((10,)), pltpu.SemaphoreType.DMA((7,))]
+        + [sems] * 6,
+        compiler_params=pltpu.CompilerParams(
+            collective_id=0, has_side_effects=True, vmem_limit_bytes=62 << 20
+        ),
+        cost_estimate=pl.CostEstimate(flops=60 * 10**9, bytes_accessed=40 << 20, transcendentals=0),
+    )(route, *gains, up_bias, down_bias, *big)
     shared_in = [
         route, x, memory, grad,
         gains[0], gains[1], self_project, self_output,
         gains[2], gains[3], cross_query, cross_memory, cross_output,
         gains[4], gains[5],
     ]
-    saved = call(
-        functools.partial(front_kernel, group_rows),
-        shared_in,
-        [
-            ((rows, 3 * width), BF),
-            ((rows, width), BF),
-            ((width, rows), BF),
-            ((PAIRS, 8, rows), F32),
-            ((rows, width), F32),
-            ((rows, width), BF),
-            ((memory.shape[0], 2 * width), BF),
-            ((rows, width), BF),
-            ((width, rows), BF),
-            ((PAIRS, 8, rows), F32),
-            ((rows, width), F32),
-            ((slot_rows, width), BF),
-            ((slot_rows, width), BF),
-        ],
-        scalars=1,
-        flops=30 * 10**9,
+    saved = [saved, total1, hidden1, total2, hidden2]
+    own = lax.axis_index("exp")
+    order = jnp.stack([partner_of(own, jnp.int32(n), size) for n in range(size)])
+    returned = lax.all_to_all(
+        jnp.take(rows_out.reshape(size, slot_rows // size, width), order, 0), "exp", split_axis=0, concat_axis=0, tiled=True
     )
-    send, send_grad = saved[-2:]
-    saved = list(saved[:-2])
-    hidden2 = saved[-1]
-
-    def exchange(values):
-        return lax.all_to_all(
-            values.reshape(size, slot_rows // size, width), "exp", split_axis=0, concat_axis=0, tiled=True
-        ).reshape(slot_rows, width)
-
-    received_grad = exchange(send_grad)
-    received = exchange(send)
-    rows_out, grad_rows, grad_up, grad_up_bias, grad_down, grad_down_bias = call(
-        experts_kernel,
-        [received, received_grad, expert_up[0], up_bias, expert_down[0], down_bias],
-        [
-            ((slot_rows, width), BF),
-            ((slot_rows, width), BF),
-            ((width, wide), BF),
-            ((1, wide), BF),
-            ((wide, width), BF),
-            ((1, width), BF),
-        ],
-        [
-            ((slot_rows, wide), BF),
-            ((slot_rows, wide), BF),
-            ((width + 16, slot_rows), BF),
-            ((width, slot_rows), BF),
-        ],
-        flops=26 * 10**9,
-    )
-    returned_grad = exchange(grad_rows)
-    returned = exchange(rows_out)
+    returned = jnp.take(returned, order, 0).reshape(slot_rows, width)
     expert_sums = (
         lax.psum_scatter(grad_up, "batch", scatter_dimension=0, tiled=True).astype(F32),
         lax.psum_scatter(grad_up_bias, "batch", scatter_dimension=1, tiled=True).astype(F32),
@@ -617,7 +750,7 @@
     )
     mats = 8
     grad_input, grad_memory, grads = call(
-        functools.partial(back_kernel, group_rows),
+        functools.partial(back_kernel, size, group_rows),
         shared_in + saved + [returned_grad],
         [
             ((rows, width), F32),
@@ -639,7 +772,7 @@
         flops=60 * 10**9,
     )
     layer_output = call(
-        functools.partial(output_kernel, group_rows),
+        functools.partial(output_kernel, size, group_rows),
         [route, hidden2, returned],
         [((rows, width), BF)],
         scalars=1,

time: 418 us -> 344 us (0.82)
  blocking collectives: 59.5 us -> 0 us
  waiting for transfers between devices: 171 us -> 142 us
  Pallas kernels: 143 us -> 154 us
  other arithmetic: 8.02 us -> 12.9 us
    pallas_call x0 -> x1, Pallas kernels: none -> 87.6 us  [body(): pl.pallas_call(functools.partial(forward_kernel, size, group_rows), out_s...]
    pallas_call x4 -> x2, Pallas kernels: 143 us -> 66.6 us  [call(): pl.pallas_call(kernel, out_shape=tuple((jax.ShapeDtypeStruct(shape, dtype...]
    all_to_all x2 -> x0, blocking collectives: 59.5 us -> none  [exchange(): lax.all_to_all(values.reshape(size, slot_rows // size, width), 'exp', spl...]
    all_to_all x2 -> x1, waiting for transfers between devices: 50.8 us -> 27.4 us  [body(): lax.all_to_all(jnp.take(rows_out.reshape(size, slot_rows // size, width),...]
    psum x1, waiting for transfers between devices: 119 us -> 114 us  [body(): grads = lax.psum(grads, ('batch', 'exp')).astype(F32)]
    select_n x0 -> x2, other arithmetic: none -> 4.77 us  [the longest x1 3.18 us: body(): returned = jnp.take(returned, order, 0).reshape(slot_rows, width)]
    gather x0 -> x2, local copies, waits for them, and re-layouts: none -> 4.27 us  [the longest x1 2.27 us: body(): jnp.take(rows_out.reshape(size, slot_rows // size, width), order, 0)]
  transfers between devices with their start and end apart: 7 -> 6, of which waited for: 3 -> 2; matrix products, arithmetic and copies ran while one was open for 4% -> 7% of each run, Pallas kernels for 16% -> 19%
where the time goes in v2:
time: 344 us
  Pallas kernels  154 us (45%)
  waiting for transfers between devices  142 us (41%)
  between operations  15.3 us (4%)
  local copies, waits for them, and re-layouts  15.2 us (4%)
  other arithmetic  12.9 us (4%)
  starting transfers between devices  3.81 us (1%)
    psum x1, waiting for transfers between devices, body(): grads = lax.psum(grads, ('batch', 'exp')).astype(F32)  114 us
    pallas_call x1, Pallas kernels, body(): pl.pallas_call(functools.partial(forward_kernel, size, group_rows), out_s...  87.6 us
    pallas_call x2, Pallas kernels, call(): pl.pallas_call(kernel, out_shape=tuple((jax.ShapeDtypeStruct(shape, dtype...  66.6 us
    all_to_all x1, waiting for transfers between devices, body(): lax.all_to_all(jnp.take(rows_out.reshape(size, slot_rows // size, width),...  27.4 us
  transfers between devices with their start and end apart: 6, of which 2 were waited for; matrix products, arithmetic and copies ran while one was open for 7% of the time, Pallas kernels for 19%

profile of v2, /device:TPU:0, one launch (start us, length us, event | category | flops | bytes accessed | tf_op | source)
XLA Modules:
  0.0 343.5 jit_solution(8768245099576263944)
XLA Ops:
  8.0 0.0 reduce-scatter.15.cloned.1.call-start
  8.1 87.6 %shard_map.322 = (bf16[10240,512]{1,0:T(8,128)(2,1)}, f32[1024,512]{1,0:T(8,128)}, f32[1024,512]{1,0:T(8,128)}, bf16[2048,512]{1,0:T(8,128)(2,1)}, bf16[2048,512...) custom-call(s32[8]{0:T(128)} %bitcast.50, ...), custom_call_target="tpu_custom_call" | custom-call | flops 60000002048 | bytes 41943040 | tf_op jit(solution)/shard_map/pallas_call | solution.py:691
  95.6 1.5 copy.39
  97.2 0.0 reduce-scatter.13.cloned.1.call-start
  97.2 1.8 copy.37
  99.0 0.0 all-reduce.2.cloned.1.call-start
  99.0 62.7 %shard_map.324 = (f32[1024,512]{1,0:T(8,128)}, f32[1024,512]{1,0:T(8,128)}, bf16[4112,512]{1,0:T(8,128)(2,1)}) custom-call(s32[8]{0:T(128)} %bitcast.51, bf16[1024,512]{1,0:T(8,128)(2,1)} %bitcast.56, bf16[1024,512]{1,0:T(8,128)(2,1)} %bitcast.58, bf16[1024,512]{1,0:T(8,128)(2,1)} %bitcast.60, f32[1,512]{1,0:T(1,128)} %bitcast.62, f32[1,512]{1,0:T(1,128)} %bitcast.64, ...), custom_call_target="tpu_custom_call" | custom-call | flops 60000002048 | bytes 20971520 | tf_op jit(solution)/shard_map/pallas_call | solution.py:639
  161.7 0.0 all-reduce.2.cloned.1.call-update
  161.8 0.0 reduce-scatter.11.cloned.1.call-start
  161.8 0.7 reduce-scatter.11.cloned.1.call-update
  162.5 0.0 reduce-scatter.9.cloned.1.call-start
  162.5 0.5 reduce-scatter.9.cloned.1.call-update
  163.1 0.1 compare_and_fusion
  163.2 2.3 gather_fusion
  165.5 1.6 broadcast_select_fusion
  167.1 3.6 %all-to-all-start = ((bf16[4,512,512]{2,1,0:T(8,128)(2,1)}), bf16[4,512,512]{2,1,0:T(8,128)(2,1)S(1)}, u32[]{:S(2)}, u32[]{:S(2)}) async-start(bf16[4,512,512]{2,1,0:T(8,128)(2,1)} %broadcast_select_fusion), calls=%async_computation | async-start | bytes 4194304 | tf_op jit(solution)/shard_map/all_to_all | solution.py:741
  170.7 0.0 reduce-scatter.15.cloned.1.call-done
  170.7 0.8 copy.40
  171.5 0.5 convert_element_type.13
  172.0 0.9 copy.38
  173.0 0.6 convert_element_type.12
  173.5 27.4 %all-to-all-done = bf16[4,512,512]{2,1,0:T(8,128)(2,1)S(1)} async-done(((bf16[4,512,512]{2,1,0:T(8,128)(2,1)}), bf16[4,512,512]{2,1,0:T(8,128)(2,1)S(1)}, u32[]{:S(2)}, u32[]{:S(2)}) %all-to-all-start) | async-done | bytes 2097184 | tf_op jit(solution)/shard_map/all_to_all | solution.py:741
  200.9 2.0 gather_fusion.1
  202.9 3.2 broadcast_select_fusion.1
  206.1 3.9 %shard_map.323 = bf16[1024,512]{1,0:T(8,128)(2,1)} custom-call(s32[8]{0:T(128)} %bitcast.52, f32[1024,512]{1,0:T(8,128)} %get-tuple-element.33.hidden2, bf16[2048,512]{1,0:T(8,128)(2,1)} %bitcast.37), custom_call_target="tpu_custom_call" | custom-call | flops 1000000 | bytes 20971520 | tf_op jit(solution)/shard_map/pallas_call | solution.py:639
  210.0 113.6 %all-reduce.2.cloned.1.call-done = bf16[4112,512]{1,0:T(8,128)(2,1)} async-done(((bf16[4112,512]{1,0:T(8,128)(2,1)}), bf16[4112,512]{1,0:T(8,128)(2,1)}) %all-reduce.2.cloned.1.call-update) | async-done | bytes 4210704 | tf_op jit(solution)/shard_map/psum | solution.py:781
  323.5 4.4 %fusion.1 = (f32[512,512]{1,0:T(8,128)}, f32[512,512]{1,0:T(8,128)S(1)}, f32[512,512]{1,0:T(8,128)S(1)}, f32[512,512]{1,0:T(8,128)}, f32[512,512]{1,0:T(8,128)},...) fusion(bf16[4112,512]{1,0:T(8,128)(2,1)} %all-reduce.2.cloned.1.call-done), kind=kLoop, calls=%fused_computation.12 | loop fusion | bytes 16777216 | tf_op jit(solution)/shard_map/slice | solution.py:782
  328.0 1.5 pad_maximum_fusion.1
  329.4 1.5 fusion
  331.0 1.9 pad_maximum_fusion
  332.8 1.8 bitcast_convert_fusion
  334.6 1.8 bitcast_convert_fusion.1
  (6 shorter events, 0.0 us)
Async XLA Ops:
  8.0 162.7 %reduce-scatter.15.cloned.1.call-start = ((), (), s32[]{:S(2)}) async-start(), calls=%async_computation.9 | async-start | bytes 147456
  97.2 74.9 %reduce-scatter.13.cloned.1.call-start = ((), (), s32[]{:S(2)}) async-start(), calls=%async_computation.8 | async-start | bytes 589824
  99.0 224.6 %all-reduce.2.cloned.1.call-start = ((), (), s32[]{:S(2)}) async-start(), calls=%async_computation.5 | async-start | bytes 8421376 | tf_op jit(solution)/shard_map/psum | solution.py:781
  161.8 171.1 %reduce-scatter.11.cloned.1.call-start = ((), (), s32[]{:S(2)}) async-start(), calls=%async_computation.7 | async-start | bytes 2359296 | tf_op jit(solution)/shard_map/reduce_scatter | solution.py:748
  162.5 172.1 %reduce-scatter.9.cloned.1.call-start = ((), (), s32[]{:S(2)}) async-start(), calls=%async_computation.6 | async-start | bytes 2359296 | tf_op jit(solution)/shard_map/reduce_scatter | solution.py:746
  167.1 33.8 %all-to-all-start = ((bf16[4,512,512]{2,1,0:T(8,128)(2,1)}), bf16[4,512,512]{2,1,0:T(8,128)(2,1)S(1)}, u32[]{:S(2)}, u32[]{:S(2)}) async-start(bf16[4,512,512]{2,1,0:T(8,128)(2,1)} %broadcast_select_fusion), calls=%async_computation | async-start | bytes 4194304 | tf_op jit(solution)/shard_map/all_to_all | solution.py:741
Sparse Core Ops, SparseCore 0:
  97.3 30.5 reduce-scatter.14
  130.7 29.1 reduce-scatter.12
  165.0 45.9 reduce-scatter.10
  213.2 37.6 reduce-scatter.8
Sparse Core Ops, SparseCore 1:
  161.8 161.7 all-reduce.1

commit v3 on v2

--- a/solution.py
+++ b/solution.py
@@ -119,7 +119,7 @@
 
 
 def attend_back(
-    query, keys, values, grad_out, out, total, grad_query, grad_keys, grad_values, sums, causal, block
+    query, keys, values, grad_out, out, total, grad_query, grad_keys, grad_values, sums, causal, block, hook=None
 ):
     rows = grad_out.shape[0]
     count = rows // block
@@ -193,6 +193,8 @@
         second(*before)
         grad_keys[0][:, columns(grad_keys[1])] = (sums[0][...] * SCALE).astype(BF)
         grad_values[0][:, columns(grad_values[1])] = sums[1][...].astype(BF)
+        if hook is not None:
+            hook(hp)
         return 0
 
     lax.fori_loop(0, PAIRS, pair, 0)
@@ -252,11 +254,11 @@
 ):
     (
         x_h, memory_h, grad_h, project_h, output_h, query_h, memory_w_h, cross_w_h, up_h, down_h,
-        saved_o, hidden1_o, hidden2_o, rows_out_o, returned_o, grad_up_o, grad_down_o,
-        total1, total2, grad_up_bias, grad_down_bias,
+        saved_o, hidden1_o, hidden2_o, rows_out_o, returned_o, half_own_o, half_other_o,
+        total1, total2, biases,
         x, memory, grad, self_project, self_output, cross_query, cross_memory, cross_output, up, down,
-        arena, hidden1, hidden2, normed3, outbound, received, received_grad, flat_t, grad_t, grad_up, grad_down,
-        in_sems, out_sems, grad_send, grad_recv, row_send, row_recv, back_send, back_recv,
+        arena, hidden1, hidden2, normed3, outbound, received, received_grad, flat_t, grad_t, halves,
+        in_sems, out_sems, core_sems, grad_send, grad_recv, row_send, row_recv, back_send, back_recv,
     ) = refs
     rows, width = x.shape
     wide = up.shape[1]
@@ -264,6 +266,12 @@
     part_rows = CAPACITY * group_rows
     slot_rows = size * part_rows
     batch, own = lax.axis_index("batch"), lax.axis_index("exp")
+
+    layers = lax.axis_size("batch") // 2
+    half = halves.shape[0] // 2
+    piece = half // layers
+    core, other = lax.rem(batch, 2), 1 - lax.rem(batch, 2)
+    twin = (batch + other - core, own)
 
     def partner(offset):
         return (batch, partner_of(own, offset, size))
@@ -283,7 +291,8 @@
     barrier = pltpu.get_barrier_semaphore()
     for offset in range(1, size):
         pl.semaphore_signal(barrier, inc=1, device_id=partner(offset), device_id_type=MESH)
-    pl.semaphore_wait(barrier, size - 1)
+    pl.semaphore_signal(barrier, inc=1, device_id=twin, device_id_type=MESH)
+    pl.semaphore_wait(barrier, size)
 
     def part(ref, offset):
         return ref.at[pl.ds(pl.multiple_of(offset * part_rows, part_rows), part_rows)]
@@ -439,27 +448,52 @@
         return bias + jnp.sum(grads.astype(F32), 0, keepdims=True)
 
     bias = lax.fori_loop(0, slot_rows // block_rows, block, jnp.zeros((1, width), F32))
-    grad_down_bias[...] = bias.astype(BF)
     stores.append(
         pltpu.make_async_copy(part(received_grad, 0), part(returned_o, 0), out_sems.at[3])
     )
     stores.append(pltpu.make_async_copy(received, rows_out_o, out_sems.at[4]))
     stores[3].start()
     stores[4].start()
+    up_rows, down_rows = width // (2 * layers), wide // (2 * layers)
+    biases[...] = jnp.zeros_like(biases)
+    per_chunk = chunk // down_rows
+
+    def piece_at(number, start, length):
+        row = lax.rem(number, 2) * half + number // 2 * piece + start
+        return halves.at[pl.ds(pl.multiple_of(row, length), length)]
 
     def weights(c, _):
         cols = span(c, chunk)
         both = nn(flat_t[...], pre_at(c, 0, slot_rows)[...])
-        grad_up[:, cols] = both[:width].astype(BF)
-        grad_up_bias[:, cols] = both[width : width + 1].astype(BF)
-        grad_down[cols] = nn(grad_t[...], hidden_at(c, 0, slot_rows)[...]).T.astype(BF)
+        for n in range(2 * layers):
+            piece_at(jnp.int32(n), c * up_rows, up_rows)[...] = both[
+                n * up_rows : (n + 1) * up_rows
+            ].astype(BF)
+        biases[pl.ds(c, 1)] = both[width : width + 1]
+        down_t = nn(grad_t[...], hidden_at(c, 0, slot_rows)[...])
+        for n in range(per_chunk):
+            piece_at(c * per_chunk + n, wide // chunk * up_rows, down_rows)[...] = down_t[
+                :, n * down_rows : (n + 1) * down_rows
+            ].T.astype(BF)
         return 0
 
     lax.fori_loop(0, wide // chunk, weights, 0)
-    stores.append(pltpu.make_async_copy(grad_up, grad_up_o, out_sems.at[5]))
-    stores.append(pltpu.make_async_copy(grad_down, grad_down_o, out_sems.at[6]))
+    biases[wide // chunk : wide // chunk + 1] = bias
+
+    def half_at(which):
+        return halves.at[pl.ds(pl.multiple_of(which * half, half), half)]
+
+    to_twin = pltpu.make_async_remote_copy(
+        src_ref=half_at(other),
+        dst_ref=half_other_o,
+        send_sem=core_sems.at[0],
+        recv_sem=core_sems.at[1],
+        device_id=twin,
+        device_id_type=MESH,
+    )
+    to_twin.start()
+    stores.append(pltpu.make_async_copy(half_at(core), half_own_o, out_sems.at[5]))
     stores[5].start()
-    stores[6].start()
     sent(outbound, received, row_send, row_recv)
     sent(received_grad, returned_o, back_send, back_recv)
 
@@ -468,75 +502,261 @@
         return 0
 
     lax.fori_loop(1, size, arrived, 0)
+    to_twin.wait()
     for store in stores[1:]:
         store.wait()
 
 
+MATS = 8
+
+
 def back_kernel(
     size,
+    layers,
     group_rows,
     routes,
-    x,
-    memory,
-    grad,
     self_gain,
     self_shift,
-    self_project,
-    self_output,
     cross_gain,
     cross_shift,
-    cross_query,
-    cross_memory,
-    cross_output,
     moe_gain,
     moe_shift,
-    saved,
     total1,
-    hidden1,
     total2,
-    hidden2,
-    returned_grad,
-    grad_input,
-    grad_memory,
-    grads,
-    carried,
-    carried_low,
-    back_low,
-    grad_q,
-    grad_kv,
-    grad_project,
-    normed,
-    sum_a,
-    sum_b,
+    biases,
+    *refs,
 ):
+    (
+        x_h, memory_h, grad_h, project_h, output_h, query_h, memory_w_h, cross_w_h,
+        saved_h, hidden1_h, hidden2_h, returned_grad_h, rows_out_h, half_own_h, half_other_h,
+        layer_o, grad_input_o, grad_memory_o, reduced_o, returned_o,
+        small, up_o, down_o, bias_o,
+        x, memory, grad, self_project, self_output, cross_query, cross_memory, cross_output,
+        saved, hidden1, hidden2, returned,
+        carried, carried_low, back_low, grad_q, grad_kv, grad_project, normed, sum_a, sum_b,
+        grads, from_twin, from_exp, part, from_layer, shard,
+        half, from_half, from_small, from_bias,
+        in_sems, out_sems, ret_send, ret_recv, half_send, half_recv, bias_send, bias_recv,
+        small_send, small_recv, sends, recvs,
+    ) = refs
     rows, width = x.shape
+    wide = up_o.shape[1]
     blocks = rows // ROWS
+    per = ROWS // group_rows
+    part_rows = CAPACITY * group_rows
     zero = jnp.zeros((1, width), F32)
-    per = ROWS // group_rows
-    tail = grads.shape[0] - 16
-    gains = []
-    own = lax.axis_index("exp")
+    batch, own = lax.axis_index("batch"), lax.axis_index("exp")
+    core, layer = lax.rem(batch, 2), batch // 2
+    twin = (batch + 1 - 2 * core, own)
+
+    def partner(offset):
+        return (batch, partner_of(own, offset, size))
+
+    def above(offset):
+        return lax.rem(layer + offset, layers)
+
+    def column(offset):
+        return (above(offset) * 2 + core, own)
+
+    pairs = [
+        (hidden2_h, hidden2), (returned_grad_h, returned), (grad_h, grad), (cross_w_h, cross_output),
+        (half_own_h, half), (half_other_h, grad_kv), (saved_h, saved), (hidden1_h, hidden1),
+        (query_h, cross_query), (memory_w_h, cross_memory), (output_h, self_output), (memory_h, memory),
+        (x_h, x), (project_h, self_project),
+    ]
+    loads = [pltpu.make_async_copy(*pair, in_sems.at[n]) for n, pair in enumerate(pairs)]
+    for load in loads:
+        load.start()
+    barrier = pltpu.get_barrier_semaphore()
+    greeted = (
+        [twin] + [partner(n) for n in range(1, size)] + [column(n) for n in range(1, layers)]
+    )
+    for device in greeted:
+        pl.semaphore_signal(barrier, inc=1, device_id=device, device_id_type=MESH)
+    pl.semaphore_wait(barrier, len(greeted))
+
+    def remote(source, target, device, send_sem, recv_sem):
+        return pltpu.make_async_remote_copy(
+            src_ref=source,
+            dst_ref=target,
+            send_sem=send_sem,
+            recv_sem=recv_sem,
+            device_id=device,
+            device_id_type=MESH,
+        )
+
+    def start_all(copies):
+        for copy in copies:
+            copy.start()
+
+    def wait_all(copies):
+        for copy in copies:
+            copy.wait()
+
+    def slots(ref, offset):
+        return ref.at[pl.ds(offset * part_rows, part_rows)]
+
+    back_rows = [
+        remote(slots(rows_out_h, n), slots(returned_o, n), partner(n), ret_send.at[n], ret_recv.at[n])
+        for n in range(1, size)
+    ]
+    start_all(back_rows)
+    own_rows = pltpu.make_async_copy(slots(rows_out_h, 0), slots(returned_o, 0), out_sems.at[0])
+    own_rows.start()
+
     q, k, v, attn, cross_q, mk, mv, cross, attn_t, cross_t = [
         saved.at[pl.ds(n * rows, rows)] for n in range(SAVED)
     ]
+    gq, gk, gv = [grad_project.at[pl.ds(n * rows, rows)] for n in range(3)]
+    gmk, gmv = [grad_kv.at[pl.ds(n * rows, rows)] for n in range(2)]
+
+    def mat(number):
+        return slice(number * width, (number + 1) * width)
 
     def times(turned, right):
-        half = 512
+        count = 512
         return sum(
-            nn(turned[n * width : (n + 1) * width], right[n * half : (n + 1) * half])
-            for n in range(rows // half)
+            nn(turned[n * width : (n + 1) * width], right[n * count : (n + 1) * count])
+            for n in range(rows // count)
         )
+
+    def gather(source, group, place):
+        expert = partner_of(own, routes[group], size)
+        rank = lax.fori_loop(
+            0,
+            group,
+            lambda j, c: c + jnp.where(routes[j] == routes[group], 1, 0).astype(jnp.int32),
+            jnp.int32(0),
+        )
+        slot = expert * CAPACITY + rank
+        total = None
+        for n in range(size * CAPACITY):
+            hit = jnp.where(slot == n, 1, 0).astype(jnp.int32)
+            term = weigh(source[n * group_rows : (n + 1) * group_rows], hit)
+            total = term if total is None else total + term
+        place[span(group, group_rows)] = total
+
+    def gather_all(source, place):
+        def one(group, _):
+            gather(source, group, place)
+            return 0
+
+        lax.fori_loop(0, rows // group_rows, one, 0)
+
+    tall = grads.shape[0]
+    by_core = tall // 2
+    by_exp = by_core // size
+    split = layers if (by_exp // layers) % 16 == 0 else 1
+    by_layer = by_exp // split
+    counter = [0]
+
+    def pair_of_sems():
+        counter[0] += 1
+        return sends.at[counter[0] - 1], recvs.at[counter[0] - 1]
+
+    def reduction(first, last):
+        cols = pl.ds(first, last - first)
+
+        def lane(ref, start, length):
+            return ref.at[pl.ds(pl.multiple_of(start, length), length), cols]
+
+        mine = core * by_core
+        core_copies = [
+            remote(lane(grads, (1 - core) * by_core, by_core), from_twin.at[:, cols], twin, *pair_of_sems())
+        ]
+        exp_copies = [
+            remote(
+                lane(grads, mine + partner_of(own, n, size) * by_exp, by_exp),
+                from_exp.at[n - 1, :, cols],
+                partner(n),
+                *pair_of_sems(),
+            )
+            for n in range(1, size)
+        ]
+        at_layer = layer * by_layer if split > 1 else 0
+        layer_copies = [
+            remote(
+                lane(part, above(n) * by_layer if split > 1 else 0, by_layer),
+                from_layer.at[n - 1, :, cols],
+                column(n),
+                *pair_of_sems(),
+            )
+            for n in range(1, layers)
+        ]
+        share_copies = [
+            remote(
+                lane(shard, at_layer, by_layer),
+                lane(shard, at_layer, by_layer),
+                column(n),
+                *pair_of_sems(),
+            )
+            for n in range(1, layers)
+        ] if split > 1 else []
+        spot = mine + own * by_exp
+        out_copies = [
+            remote(shard.at[:, cols], lane(reduced_o, spot, by_exp), partner(n), *pair_of_sems())
+            for n in range(1, size)
+        ]
+        local = pltpu.make_async_copy(shard.at[:, cols], lane(reduced_o, spot, by_exp), pair_of_sems()[0])
+        half_copies = [
+            remote(lane(reduced_o, mine, by_core), lane(reduced_o, mine, by_core), twin, *pair_of_sems())
+        ]
+
+        def stage(number):
+            if number == 0:
+                start_all(core_copies)
+            if number == 1:
+                wait_all(core_copies)
+
+                def add(i, _):
+                    here = pl.ds(pl.multiple_of(mine + i * 64, 64), 64)
+                    grads[here, cols] = (
+                        grads[here, cols].astype(F32) + from_twin[span(i, 64), cols].astype(F32)
+                    ).astype(BF)
+                    return 0
+
+                lax.fori_loop(0, by_core // 64, add, 0)
+                start_all(exp_copies)
+            if number == 2:
+                wait_all(exp_copies)
+                here = pl.ds(pl.multiple_of(spot, by_exp), by_exp)
+                total = grads[here, cols].astype(F32)
+                for n in range(size - 1):
+                    total = total + from_exp[n, :, cols].astype(F32)
+                part[:, cols] = total.astype(BF)
+                start_all(layer_copies)
+            if number == 3:
+                wait_all(layer_copies)
+                here = pl.ds(pl.multiple_of(at_layer, by_layer), by_layer)
+                total = part[here, cols].astype(F32)
+                for n in range(layers - 1):
+                    total = total + from_layer[n, :, cols].astype(F32)
+                shard[here, cols] = total.astype(BF)
+                start_all(share_copies)
+            if number == 4:
+                wait_all(share_copies)
+                start_all(out_copies)
+                local.start()
+            if number == 5:
+                wait_all(out_copies)
+                local.wait()
+                start_all(half_copies)
+            if number == 6:
+                wait_all(half_copies)
+
+        return stage
+
+    late = reduction(0, 3 * width)
+    early = reduction(3 * width, MATS * width)
+
+    for load in loads[:4]:
+        load.wait()
+    gather_all(returned, carried_low)
 
     def block3(i, carry):
         here = span(i, ROWS)
         hat, scale = normalize(hidden2[here])
-        gy = jnp.concatenate(
-            [
-                returned_grad[span(slot_of(routes, i * per + part, own, size), group_rows)]
-                for part in range(per)
-            ],
-            0,
-        ).astype(F32)
+        gy = carried_low[here].astype(F32)
         total = grad[here].astype(F32) + normalize_back(hat, scale, gy, moe_gain[...])
         carried[here] = total
         low = total.astype(BF)
@@ -547,21 +767,37 @@
             carry[1] + jnp.sum(gy, 0, keepdims=True),
         )
 
-    gains.append(lax.fori_loop(0, blocks, block3, (zero, zero)))
-    grads[span(7, width)] = times(cross_t, carried_low).astype(BF)
+    gains3 = lax.fori_loop(0, blocks, block3, (zero, zero))
+
+    for load in loads[4:6]:
+        load.wait()
+
+    def add_half(i, _):
+        here = span(i, ROWS)
+        half[here] = (half[here].astype(F32) + grad_kv[here].astype(F32)).astype(BF)
+        return 0
+
+    lax.fori_loop(0, half.shape[0] // ROWS, add_half, 0)
+    piece = half.shape[0] // layers
+    pieces = [
+        remote(
+            half.at[pl.ds(pl.multiple_of(above(n) * piece, piece), piece)],
+            from_half.at[n - 1],
+            column(n),
+            half_send.at[n],
+            half_recv.at[n],
+        )
+        for n in range(1, layers)
+    ]
+    start_all(pieces)
+    bias_twin = [remote(biases, from_bias.at[0], twin, bias_send.at[0], bias_recv.at[0])]
+    start_all(bias_twin)
+    for load in loads[6:]:
+        load.wait()
+    grads[:, mat(7)] = times(cross_t, carried_low).astype(BF)
     attend_back(
-        (cross_q, 0),
-        (mk, 0),
-        (mv, 0),
-        back_low,
-        cross,
-        total2,
-        (grad_q, 0),
-        (grad_kv, 0),
-        (grad_kv, width),
-        (sum_a, sum_b),
-        False,
-        256,
+        (cross_q, 0), (mk, 0), (mv, 0), back_low, cross, total2,
+        (grad_q, 0), (gmk, 0), (gmv, 0), (sum_a, sum_b), False, 256,
     )
 
     def block2(i, carry):
@@ -574,77 +810,151 @@
         low = total.astype(BF)
         carried_low[here] = low
         back_low[here] = nt(low, self_output[...]).astype(BF)
-        grad_memory[here] = nt(grad_kv[here], cross_memory[...])
         return (
             carry[0] + jnp.sum(gy * hat, 0, keepdims=True),
             carry[1] + jnp.sum(gy, 0, keepdims=True),
         )
 
-    gains.append(lax.fori_loop(0, blocks, block2, (zero, zero)))
-    grads[span(4, width)] = tn(normed[...], grad_q[...]).astype(BF)
-    grads[span(5, width)] = tn(memory[...], grad_kv[:, :width]).astype(BF)
-    grads[span(6, width)] = tn(memory[...], grad_kv[:, width:]).astype(BF)
-    grads[span(3, width)] = times(attn_t, carried_low).astype(BF)
+    gains2 = lax.fori_loop(0, blocks, block2, (zero, zero))
+    grads[:, mat(4)] = tn(normed[...], grad_q[...]).astype(BF)
+    grads[:, mat(5)] = tn(memory[...], gmk[...]).astype(BF)
+    grads[:, mat(6)] = tn(memory[...], gmv[...]).astype(BF)
+    grads[:, mat(3)] = times(attn_t, carried_low).astype(BF)
+    early(0)
+    wait_all(bias_twin)
+    biases[...] += from_bias[0]
+    bias_layers = [
+        remote(biases, from_bias.at[n], column(n), bias_send.at[n], bias_recv.at[n])
+        for n in range(1, layers)
+    ]
+    start_all(bias_layers)
+
+    def hook(hp):
+        @pl.when(hp == 0)
+        def _():
+            early(1)
+
     attend_back(
-        (q, 0),
-        (k, 0),
-        (v, 0),
-        back_low,
-        attn,
-        total1,
-        (grad_project, 0),
-        (grad_project, width),
-        (grad_project, 2 * width),
-        (sum_a, sum_b),
-        True,
-        256,
+        (q, 0), (k, 0), (v, 0), back_low, attn, total1,
+        (gq, 0), (gk, 0), (gv, 0), (sum_a, sum_b), True, 256, hook,
     )
+    early(2)
+
+    def renormed(i, _):
+        here = span(i, ROWS)
+        hat, _s = normalize(x[here].astype(F32))
+        normed[here] = (hat * self_gain[...] + self_shift[...]).astype(BF)
+        return 0
+
+    lax.fori_loop(0, blocks, renormed, 0)
+    for n, ref in enumerate((gq, gk, gv)):
+        grads[:, mat(n)] = tn(normed[...], ref[...]).astype(BF)
+    late(0)
+    early(3)
 
     def block1(i, carry):
         here = span(i, ROWS)
         hat, scale = normalize(x[here].astype(F32))
-        normed[here] = (hat * self_gain[...] + self_shift[...]).astype(BF)
-        gy = nt(grad_project[here], self_project[...])
-        grad_input[here] = carried[here] + normalize_back(hat, scale, gy, self_gain[...])
+        gy = sum(
+            nt(ref[here], self_project[:, mat(n)]) for n, ref in enumerate((gq, gk, gv))
+        )
+        carried[here] += normalize_back(hat, scale, gy, self_gain[...])
         return (
             carry[0] + jnp.sum(gy * hat, 0, keepdims=True),
             carry[1] + jnp.sum(gy, 0, keepdims=True),
         )
 
-    gains.append(lax.fori_loop(0, blocks, block1, (zero, zero)))
-    for part in range(3):
-        grads[span(part, width)] = tn(
-            normed[...], grad_project[:, part * width : (part + 1) * width]
-        ).astype(BF)
-    small = [gains[2][0], gains[2][1], gains[1][0], gains[1][1], gains[0][0], gains[0][1]]
-    grads[tail:] = jnp.concatenate(small + [jnp.zeros((10, width), F32)], 0).astype(BF)
-
-
-def output_kernel(size, group_rows, routes, hidden2, returned, out):
-    own = lax.axis_index("exp")
-    groups = out.shape[0] // group_rows
-
-    def block(i, _):
-        here = span(i, group_rows)
-        moved = returned[span(slot_of(routes, i, own, size), group_rows)]
-        out[here] = (hidden2[here] + moved.astype(F32)).astype(BF)
+    gains1 = lax.fori_loop(0, blocks, block1, (zero, zero))
+    stores = [pltpu.make_async_copy(carried, grad_input_o, out_sems.at[1])]
+    stores[0].start()
+    late(1)
+    early(4)
+    small[...] = jnp.concatenate([*gains1, *gains2, *gains3, zero, zero], 0)
+
+    def share_small(number, devices):
+        copies = [
+            remote(small, from_small.at[number + n], device, small_send.at[number + n], small_recv.at[number + n])
+            for n, device in enumerate(devices)
+        ]
+        start_all(copies)
+
+        def finish():
+            wait_all(copies)
+            total = small[...]
+            for n in range(len(devices)):
+                total = total + from_small[number + n]
+            small[...] = total
+
+        return finish
+
+    finish = share_small(0, [twin])
+
+    wait_all(back_rows)
+    own_rows.wait()
+    fetch = pltpu.make_async_copy(returned_o, returned, out_sems.at[2])
+    fetch.start()
+    finish()
+    finish = share_small(1, [partner(n) for n in range(1, size)])
+
+    def memory_block(i, _):
+        here = span(i, ROWS)
+        hidden1[here] = nt(gmk[here], cross_memory[:, :width]) + nt(gmv[here], cross_memory[:, width:])
         return 0
 
-    lax.fori_loop(0, groups, block, 0)
-
-
-def call(kernel, inputs, outputs, scratch=(), scalars=0, flops=0):
-    vmem = pl.BlockSpec(memory_space=pltpu.VMEM)
-    smem = pl.BlockSpec(memory_space=pltpu.SMEM)
-    return pl.pallas_call(
-        kernel,
-        out_shape=tuple(jax.ShapeDtypeStruct(shape, dtype) for shape, dtype in outputs),
-        in_specs=[smem] * scalars + [vmem] * (len(inputs) - scalars),
-        out_specs=tuple(vmem for _ in outputs),
-        scratch_shapes=[pltpu.VMEM(shape, dtype) for shape, dtype in scratch],
-        compiler_params=pltpu.CompilerParams(vmem_limit_bytes=60 << 20),
-        cost_estimate=pl.CostEstimate(flops=flops, bytes_accessed=20 << 20, transcendentals=0),
-    )(*inputs)
+    lax.fori_loop(0, rows // ROWS, memory_block, 0)
+    stores.append(pltpu.make_async_copy(hidden1, grad_memory_o, out_sems.at[3]))
+    stores[1].start()
+    fetch.wait()
+    gather_all(returned, normed)
+
+    def output_block(i, _):
+        here = span(i, ROWS)
+        grad[here] = (hidden2[here] + normed[here].astype(F32)).astype(BF)
+        return 0
+
+    lax.fori_loop(0, blocks, output_block, 0)
+    stores.append(pltpu.make_async_copy(grad, layer_o, out_sems.at[4]))
+    stores[2].start()
+    finish()
+    finish = share_small(size, [column(n) for n in range(1, layers)])
+    late(2)
+    early(5)
+    wait_all(pieces)
+    up_rows = up_o.shape[0]
+    base = layer * piece
+    for c in range(wide // width):
+        total = half[pl.ds(pl.multiple_of(base + c * up_rows, up_rows), up_rows)].astype(F32)
+        for n in range(layers - 1):
+            total = total + from_half[n, c * up_rows : (c + 1) * up_rows].astype(F32)
+        up_o[:, c * width : (c + 1) * width] = total
+    down_rows = down_o.shape[0]
+    start = wide // width * up_rows
+    total = half[pl.ds(pl.multiple_of(base + start, down_rows), down_rows)].astype(F32)
+    for n in range(layers - 1):
+        total = total + from_half[n, start : start + down_rows].astype(F32)
+    down_o[...] = total
+    wait_all(bias_layers)
+    total = biases[...]
+    for n in range(1, layers):
+        total = total + from_bias[n]
+    bias_o[...] = total
+    late(3)
+    early(6)
+    finish()
+    late(4)
+    late(5)
+    late(6)
+    for store in stores:
+        store.wait()
+
+
+def finish_kernel(reduced, project, output, query, memory, cross):
+    width = output.shape[1]
+    column = 0
+    for target in (project, output, query, memory, cross):
+        size = target.shape[1]
+        target[...] = reduced[:, column : column + size].astype(F32)
+        column += size
 
 
 def body(
@@ -688,7 +998,7 @@
         expert_up[0], expert_down[0],
     ]
     sems = pltpu.SemaphoreType.DMA((size,))
-    saved, hidden1, hidden2, rows_out, returned_grad, grad_up, grad_down, total1, total2, grad_up_bias, grad_down_bias = pl.pallas_call(
+    saved, hidden1, hidden2, rows_out, returned_grad, half_own, half_other, total1, total2, biases = pl.pallas_call(
         functools.partial(forward_kernel, size, group_rows),
         out_shape=(
             array((SAVED * rows, width), BF),
@@ -696,15 +1006,14 @@
             array((rows, width), F32),
             array((slot_rows, width), BF),
             array((slot_rows, width), BF),
-            array((width, wide), BF),
+            array((wide, width), BF),
             array((wide, width), BF),
             array((PAIRS, 8, rows), F32),
             array((PAIRS, 8, rows), F32),
-            array((1, wide), BF),
-            array((1, width), BF),
+            array((8, width), F32),
         ),
         in_specs=[smem] + [vmem] * 8 + [any_] * 10,
-        out_specs=(any_,) * 7 + (vmem,) * 4,
+        out_specs=(any_,) * 7 + (vmem,) * 3,
         scratch_shapes=[pltpu.VMEM(v.shape, v.dtype) for v in big]
         + [
             pltpu.VMEM(shape, dtype)
@@ -718,88 +1027,115 @@
                 ((slot_rows, width), BF),
                 ((width + 16, slot_rows), BF),
                 ((width, slot_rows), BF),
-                ((width, wide), BF),
-                ((wide, width), BF),
+                ((2 * wide, width), BF),
             ]
         ]
-        + [pltpu.SemaphoreType.DMA((10,)), pltpu.SemaphoreType.DMA((7,))]
+        + [pltpu.SemaphoreType.DMA((10,)), pltpu.SemaphoreType.DMA((6,)), pltpu.SemaphoreType.DMA((2,))]
         + [sems] * 6,
         compiler_params=pltpu.CompilerParams(
             collective_id=0, has_side_effects=True, vmem_limit_bytes=62 << 20
         ),
         cost_estimate=pl.CostEstimate(flops=60 * 10**9, bytes_accessed=40 << 20, transcendentals=0),
     )(route, *gains, up_bias, down_bias, *big)
-    shared_in = [
-        route, x, memory, grad,
-        gains[0], gains[1], self_project, self_output,
-        gains[2], gains[3], cross_query, cross_memory, cross_output,
-        gains[4], gains[5],
+    layers = lax.axis_size("batch") // 2
+    by_exp = width // 2 // size
+    by_layer = by_exp // layers if (by_exp // layers) % 16 == 0 else by_exp
+    piece = wide // layers
+    back_in = [
+        *big[:8], saved, hidden1, hidden2, returned_grad, rows_out, half_own, half_other,
     ]
-    saved = [saved, total1, hidden1, total2, hidden2]
-    own = lax.axis_index("exp")
-    order = jnp.stack([partner_of(own, jnp.int32(n), size) for n in range(size)])
-    returned = lax.all_to_all(
-        jnp.take(rows_out.reshape(size, slot_rows // size, width), order, 0), "exp", split_axis=0, concat_axis=0, tiled=True
+    count = 2 * (4 + 2 * (size - 1) + 2 * (layers - 1))
+    dma = pltpu.SemaphoreType.DMA
+    (
+        layer_output, grad_input, grad_memory, reduced, _returned, small, grad_up, grad_down, biases,
+    ) = pl.pallas_call(
+        functools.partial(back_kernel, size, layers, group_rows),
+        out_shape=(
+            array((rows, width), BF),
+            array((rows, width), F32),
+            array((rows, width), F32),
+            array((width, MATS * width), BF),
+            array((slot_rows, width), BF),
+            array((8, width), F32),
+            array((width // (2 * layers), wide), F32),
+            array((wide // (2 * layers), width), F32),
+            array((8, width), F32),
+        ),
+        in_specs=[smem] + [vmem] * 9 + [any_] * len(back_in),
+        out_specs=(any_,) * 5 + (vmem,) * 4,
+        scratch_shapes=[pltpu.VMEM(v.shape, v.dtype) for v in big[:8]]
+        + [
+            pltpu.VMEM(shape, dtype)
+            for shape, dtype in [
+                (saved.shape, BF),
+                ((rows, width), F32),
+                ((rows, width), F32),
+                ((slot_rows, width), BF),
+                ((rows, width), F32),
+                ((rows, width), BF),
+                ((rows, width), BF),
+                ((rows, width), BF),
+                ((2 * rows, width), BF),
+                ((3 * rows, width), BF),
+                ((rows, width), BF),
+                ((rows, PAIR), F32),
+                ((rows, PAIR), F32),
+                ((width, MATS * width), BF),
+                ((width // 2, MATS * width), BF),
+                ((size - 1, by_exp, MATS * width), BF),
+                ((by_exp, MATS * width), BF),
+                ((layers - 1, by_layer, MATS * width), BF),
+                ((by_exp, MATS * width), BF),
+                ((wide, width), BF),
+                ((layers - 1, piece, width), BF),
+                ((size + layers - 1, 8, width), F32),
+                ((layers, 8, width), F32),
+            ]
+        ]
+        + [dma((14,)), dma((5,)), sems, sems]
+        + [dma((layers,))] * 4
+        + [dma((size + layers - 1,))] * 2
+        + [dma((count,))] * 2,
+        compiler_params=pltpu.CompilerParams(
+            collective_id=1, has_side_effects=True, vmem_limit_bytes=63 << 20
+        ),
+        cost_estimate=pl.CostEstimate(flops=60 * 10**9, bytes_accessed=40 << 20, transcendentals=0),
+    )(route, *gains, total1, total2, biases, *back_in)
+    shapes = [(width, 3 * width), (width, width), (width, width), (width, 2 * width), (width, width)]
+    steps = 4
+    grad_self_project, grad_self_output, grad_cross_query, grad_cross_memory, grad_cross_output = pl.pallas_call(
+        finish_kernel,
+        grid=(steps,),
+        out_shape=tuple(array(shape, F32) for shape in shapes),
+        in_specs=[pl.BlockSpec((width // steps, MATS * width), lambda i: (i, 0))],
+        out_specs=tuple(pl.BlockSpec((width // steps, shape[1]), lambda i: (i, 0)) for shape in shapes),
+    )(reduced)
+    index = lax.axis_index("batch")
+    up_bias_sum = lax.dynamic_slice_in_dim(
+        biases[: wide // width].reshape(1, wide), index * (wide // (2 * layers)), wide // (2 * layers), 1
     )
-    returned = jnp.take(returned, order, 0).reshape(slot_rows, width)
-    expert_sums = (
-        lax.psum_scatter(grad_up, "batch", scatter_dimension=0, tiled=True).astype(F32),
-        lax.psum_scatter(grad_up_bias, "batch", scatter_dimension=1, tiled=True).astype(F32),
-        lax.psum_scatter(grad_down, "batch", scatter_dimension=0, tiled=True).astype(F32),
-        lax.psum_scatter(grad_down_bias, "batch", scatter_dimension=1, tiled=True).astype(F32),
+    down_bias_sum = lax.dynamic_slice_in_dim(
+        biases[wide // width : wide // width + 1], index * (width // (2 * layers)), width // (2 * layers), 1
     )
-    mats = 8
-    grad_input, grad_memory, grads = call(
-        functools.partial(back_kernel, size, group_rows),
-        shared_in + saved + [returned_grad],
-        [
-            ((rows, width), F32),
-            ((memory.shape[0], width), F32),
-            ((mats * width + 16, width), BF),
-        ],
-        [
-            ((rows, width), F32),
-            ((rows, width), BF),
-            ((rows, width), BF),
-            ((rows, width), BF),
-            ((memory.shape[0], 2 * width), BF),
-            ((rows, 3 * width), BF),
-            ((rows, width), BF),
-            ((max(rows, memory.shape[0]), PAIR), F32),
-            ((max(rows, memory.shape[0]), PAIR), F32),
-        ],
-        scalars=1,
-        flops=60 * 10**9,
-    )
-    layer_output = call(
-        functools.partial(output_kernel, size, group_rows),
-        [route, hidden2, returned],
-        [((rows, width), BF)],
-        scalars=1,
-        flops=10**6,
-    )[0]
-    grads = lax.psum(grads, ("batch", "exp")).astype(F32)
-    mat = [grads[i * width : (i + 1) * width] for i in range(mats)]
-    small = grads[mats * width :]
     return (
         layer_output[None],
         grad_input[None],
         grad_memory[None],
         small[0],
         small[1],
-        jnp.concatenate(mat[0:3], 1),
-        mat[3],
+        grad_self_project,
+        grad_self_output,
         small[2],
         small[3],
-        mat[4],
-        jnp.concatenate(mat[5:7], 1),
-        mat[7],
+        grad_cross_query,
+        grad_cross_memory,
+        grad_cross_output,
         small[4],
         small[5],
-        expert_sums[0][None],
-        expert_sums[1],
-        expert_sums[2][None],
-        expert_sums[3],
+        grad_up[None],
+        up_bias_sum,
+        grad_down[None],
+        down_bias_sum,
     )
 
 

time: 344 us -> 221 us (0.64)
  waiting for transfers between devices: 142 us -> 0 us
  Pallas kernels: 154 us -> 212 us
  between operations: 15.3 us -> 0.73 us
  other arithmetic: 12.9 us -> 0 us
  local copies, waits for them, and re-layouts: 15.2 us -> 8.07 us
  starting transfers between devices: 3.81 us -> 0 us
    psum x1 -> x0, waiting for transfers between devices: 114 us -> none  [body(): grads = lax.psum(grads, ('batch', 'exp')).astype(F32)]
    pallas_call x2, Pallas kernels: 66.6 us -> 125 us  [the longest x1 119 us: body(): pl.pallas_call(functools.partial(back_kernel, size, layers, group_rows),...]
    all_to_all x1 -> x0, waiting for transfers between devices: 27.4 us -> none  [body(): lax.all_to_all(jnp.take(rows_out.reshape(size, slot_rows // size, width),...]
    select_n x2 -> x0, other arithmetic: 4.77 us -> none  [the longest x1 3.18 us: body(): returned = jnp.take(returned, order, 0).reshape(slot_rows, width)]
    slice x1, local copies, waits for them, and re-layouts: 4.43 us -> 0.01 us  [body(): biases[wide // width:wide // width + 1]]
    gather x2 -> x0, local copies, waits for them, and re-layouts: 4.27 us -> none  [the longest x1 2.27 us: body(): jnp.take(rows_out.reshape(size, slot_rows // size, width), order, 0)]
    all_to_all x1 -> x0, starting transfers between devices: 3.61 us -> none  [body(): lax.all_to_all(jnp.take(rows_out.reshape(size, slot_rows // size, width),...]
    broadcast_in_dim x2 -> x0, other arithmetic: 3.58 us -> none  [the longest x1 1.8 us: body(): expert_sums[2][None]]
  transfers between devices with their start and end apart: 6 -> 0, of which waited for: 2 -> 0; matrix products, arithmetic and copies ran while one was open for 7% -> 0% of each run, Pallas kernels for 19% -> 0%
where the time goes in v3:
time: 221 us
  Pallas kernels  212 us (96%)
  local copies, waits for them, and re-layouts  8.07 us (4%)
    pallas_call x1, Pallas kernels, body(): pl.pallas_call(functools.partial(back_kernel, size, layers, group_rows),...  119 us
    pallas_call x1, Pallas kernels, body(): pl.pallas_call(functools.partial(forward_kernel, size, group_rows), out_s...  87.6 us
    unnamed x21, local copies, waits for them, and re-layouts  6.31 us
    pallas_call x1, Pallas kernels, body(): pl.pallas_call(finish_kernel, grid=(steps,), out_shape=tuple((array(shape...  5.94 us

profile of v3, /device:TPU:0, one launch (start us, length us, event | category | flops | bytes accessed | tf_op | source)
XLA Modules:
  0.0 221.0 jit_solution(14586199180929496306)
XLA Ops:
  0.7 87.6 %shard_map.322 = (bf16[10240,512]{1,0:T(8,128)(2,1)}, f32[1024,512]{1,0:T(8,128)}, f32[1024,512]{1,0:T(8,128)}, bf16[2048,512]{1,0:T(8,128)(2,1)}, bf16[2048,512...) custom-call(s32[8]{0:T(128)} %bitcast.59, ...), custom_call_target="tpu_custom_call" | custom-call | flops 60000002048 | bytes 41943040 | tf_op jit(solution)/shard_map/pallas_call | solution.py:1001
  88.2 118.7 %shard_map.323 = (bf16[1024,512]{1,0:T(8,128)(2,1)}, f32[1024,512]{1,0:T(8,128)}, f32[1024,512]{1,0:T(8,128)}, bf16[512,4096]{1,0:T(8,128)(2,1)}, bf16[2048,512]...) custom-call(s32[8]{0:T(128)} %bitcast.60, ...), custom_call_target="tpu_custom_call" | custom-call | flops 60000002048 | bytes 41943040 | tf_op jit(solution)/shard_map/pallas_call | solution.py:1051
  206.9 0.0 copy-start.6
  207.0 0.0 copy-start.5
  207.0 0.0 copy-start.2
  207.0 5.9 %shard_map.324 = (f32[512,1536]{1,0:T(8,128)}, f32[512,512]{1,0:T(8,128)}, f32[512,512]{1,0:T(8,128)}, f32[512,1024]{1,0:T(8,128)}, f32[512,512]{1,0:T(8,128)}) custom-call(bf16[512,4096]{1,0:T(8,128)(2,1)} %get-tuple-element.55.reduced), custom_call_target="tpu_custom_call" | custom-call | tf_op jit(solution)/shard_map/pallas_call | solution.py:1106
  212.9 0.0 copy-start.1
  212.9 0.0 copy-done.6
  213.0 0.6 constant_dynamic-slice_fusion.1
  213.5 0.0 copy-done.5
  213.5 0.6 fusion
  214.1 0.6 constant_dynamic-slice_fusion
  214.7 0.0 copy-done.2
  214.7 1.0 copy.43
  215.7 0.0 copy-done.1
  215.7 0.0 copy-start
  215.7 1.3 copy.44
  217.0 1.0 copy-done
  218.1 0.0 copy-start.4
  218.1 0.0 copy-start.3
  218.1 1.3 copy.45
  219.4 0.1 copy-done.4
  219.4 0.8 copy.46
  220.2 0.0 copy-done.3
  220.2 0.8 copy.47
  (3 shorter events, 0.0 us)
Async XLA Ops:
  206.9 6.0 %copy-start.6 = (f32[8,512]{1,0:T(8,128)S(1)}, f32[8,512]{1,0:T(8,128)}, u32[]{:S(2)}) copy-start(f32[8,512]{1,0:T(8,128)} %get-tuple-element.62) | copy-start | bytes 49156
  207.0 6.6 %copy-start.5 = (f32[8,512]{1,0:T(8,128)S(1)}, f32[8,512]{1,0:T(8,128)}, u32[]{:S(2)}) copy-start(f32[8,512]{1,0:T(8,128)} %get-tuple-element.54) | copy-start | bytes 49156
  207.0 7.8 %copy-start.2 = (bf16[1024,512]{1,0:T(8,128)(2,1)S(1)}, bf16[1024,512]{1,0:T(8,128)(2,1)}, u32[]{:S(2)}) copy-start(bf16[1024,512]{1,0:T(8,128)(2,1)} %get-tuple-element.51) | copy-start | bytes 3145732
  212.9 2.8 %copy-start.1 = (f32[1024,512]{1,0:T(8,128)S(1)}, f32[1024,512]{1,0:T(8,128)}, u32[]{:S(2)}) copy-start(f32[1024,512]{1,0:T(8,128)} %get-tuple-element.52) | copy-start | bytes 6291460
  215.7 2.3 %copy-start = (f32[1024,512]{1,0:T(8,128)S(1)}, f32[1024,512]{1,0:T(8,128)}, u32[]{:S(2)}) copy-start(f32[1024,512]{1,0:T(8,128)} %get-tuple-element.53) | copy-start | bytes 6291460
  218.1 1.4 copy-start.4
  218.1 2.2 copy-start.3

commit v4 on v3

--- a/solution.py
+++ b/solution.py
@@ -534,7 +534,7 @@
         x, memory, grad, self_project, self_output, cross_query, cross_memory, cross_output,
         saved, hidden1, hidden2, returned,
         carried, carried_low, back_low, grad_q, grad_kv, grad_project, normed, sum_a, sum_b,
-        grads, from_twin, from_exp, part, from_layer, shard,
+        grads, from_twin, from_exp, part, from_layer, from_layer_whole, shard,
         half, from_half, from_small, from_bias,
         in_sems, out_sems, ret_send, ret_recv, half_send, half_recv, bias_send, bias_recv,
         small_send, small_recv, sends, recvs,
@@ -646,15 +646,17 @@
     tall = grads.shape[0]
     by_core = tall // 2
     by_exp = by_core // size
-    split = layers if (by_exp // layers) % 16 == 0 else 1
-    by_layer = by_exp // split
     counter = [0]
 
     def pair_of_sems():
         counter[0] += 1
         return sends.at[counter[0] - 1], recvs.at[counter[0] - 1]
 
-    def reduction(first, last):
+    def reduction(first, last, whole=False):
+        split = layers if (by_exp // layers) % 16 == 0 and not whole else 1
+        by_layer = by_exp // split
+        landing = from_layer_whole if whole else from_layer
+        shift = first if whole else 0
         cols = pl.ds(first, last - first)
 
         def lane(ref, start, length):
@@ -677,7 +679,7 @@
         layer_copies = [
             remote(
                 lane(part, above(n) * by_layer if split > 1 else 0, by_layer),
-                from_layer.at[n - 1, :, cols],
+                landing.at[n - 1, :, pl.ds(first - shift, last - first)],
                 column(n),
                 *pair_of_sems(),
             )
@@ -724,30 +726,36 @@
                 for n in range(size - 1):
                     total = total + from_exp[n, :, cols].astype(F32)
                 part[:, cols] = total.astype(BF)
+            if number == 3:
                 start_all(layer_copies)
-            if number == 3:
+            if number == 4:
                 wait_all(layer_copies)
                 here = pl.ds(pl.multiple_of(at_layer, by_layer), by_layer)
                 total = part[here, cols].astype(F32)
                 for n in range(layers - 1):
-                    total = total + from_layer[n, :, cols].astype(F32)
+                    total = total + landing[n, :, first - shift : last - shift].astype(F32)
                 shard[here, cols] = total.astype(BF)
                 start_all(share_copies)
-            if number == 4:
+            if number == 5:
                 wait_all(share_copies)
                 start_all(out_copies)
                 local.start()
-            if number == 5:
+            if number == 6:
                 wait_all(out_copies)
                 local.wait()
                 start_all(half_copies)
-            if number == 6:
+            if number == 7:
                 wait_all(half_copies)
 
         return stage
 
-    late = reduction(0, 3 * width)
-    early = reduction(3 * width, MATS * width)
+    per_pair = 3 * PAIR
+    part_a = reduction(7 * width, 8 * width)
+    part_b = reduction(5 * width, 7 * width)
+    first_sum = reduction(5 * width, 8 * width)
+    second_sum = reduction(3 * width, 5 * width)
+    third_sum = reduction(0, 3 * per_pair)
+    last_sum = reduction(3 * per_pair, 4 * per_pair, True)
 
     for load in loads[:4]:
         load.wait()
@@ -779,26 +787,55 @@
 
     lax.fori_loop(0, half.shape[0] // ROWS, add_half, 0)
     piece = half.shape[0] // layers
+    turns = 8
+    turn_rows = piece // turns
     pieces = [
-        remote(
-            half.at[pl.ds(pl.multiple_of(above(n) * piece, piece), piece)],
-            from_half.at[n - 1],
-            column(n),
-            half_send.at[n],
-            half_recv.at[n],
-        )
-        for n in range(1, layers)
+        [
+            remote(
+                half.at[pl.ds(pl.multiple_of(above(n) * piece + turn * turn_rows, turn_rows), turn_rows)],
+                from_half.at[n - 1, pl.ds(turn * turn_rows, turn_rows)],
+                column(n),
+                half_send.at[(n - 1) * turns + turn],
+                half_recv.at[(n - 1) * turns + turn],
+            )
+            for n in range(1, layers)
+        ]
+        for turn in range(turns)
     ]
-    start_all(pieces)
+    start_all(pieces[0])
     bias_twin = [remote(biases, from_bias.at[0], twin, bias_send.at[0], bias_recv.at[0])]
     start_all(bias_twin)
     for load in loads[6:]:
         load.wait()
     grads[:, mat(7)] = times(cross_t, carried_low).astype(BF)
+    part_a(0)
+
+    def cross_hook(hp):
+        @pl.when(hp == 0)
+        def _():
+            part_a(1)
+            start_all(pieces[1])
+
+        @pl.when(hp == 1)
+        def _():
+            start_all(pieces[2])
+
+        @pl.when(hp == 2)
+        def _():
+            start_all(pieces[3])
+
+        @pl.when(hp == 3)
+        def _():
+            start_all(pieces[4])
+            part_a(2)
+
     attend_back(
         (cross_q, 0), (mk, 0), (mv, 0), back_low, cross, total2,
-        (grad_q, 0), (gmk, 0), (gmv, 0), (sum_a, sum_b), False, 256,
+        (grad_q, 0), (gmk, 0), (gmv, 0), (sum_a, sum_b), False, 256, cross_hook,
     )
+    grads[:, mat(5)] = tn(memory[...], gmk[...]).astype(BF)
+    grads[:, mat(6)] = tn(memory[...], gmv[...]).astype(BF)
+    part_b(0)
 
     def block2(i, carry):
         here = span(i, ROWS)
@@ -816,11 +853,11 @@
         )
 
     gains2 = lax.fori_loop(0, blocks, block2, (zero, zero))
+    part_b(1)
+    start_all(pieces[5])
     grads[:, mat(4)] = tn(normed[...], grad_q[...]).astype(BF)
-    grads[:, mat(5)] = tn(memory[...], gmk[...]).astype(BF)
-    grads[:, mat(6)] = tn(memory[...], gmv[...]).astype(BF)
     grads[:, mat(3)] = times(attn_t, carried_low).astype(BF)
-    early(0)
+    second_sum(0)
     wait_all(bias_twin)
     biases[...] += from_bias[0]
     bias_layers = [
@@ -828,29 +865,47 @@
         for n in range(1, layers)
     ]
     start_all(bias_layers)
-
-    def hook(hp):
+    for n in range(rows // 512):
+        hat, _s = normalize(x[n * 512 : (n + 1) * 512].astype(F32))
+        normed[n * width : (n + 1) * width] = (
+            (hat * self_gain[...] + self_shift[...]).astype(BF).T
+        )
+
+    def self_hook(hp):
+        cols = span(hp, PAIR)
+        three = jnp.concatenate([gq[:, cols], gk[:, cols], gv[:, cols]], 1)
+        grads[:, pl.ds(pl.multiple_of(hp * per_pair, PAIR), per_pair)] = times(normed, three).astype(BF)
+
         @pl.when(hp == 0)
         def _():
-            early(1)
+            second_sum(1)
+            part_b(2)
+            first_sum(3)
+
+        @pl.when(hp == 1)
+        def _():
+            first_sum(4)
+            start_all(pieces[6])
+
+        @pl.when(hp == 2)
+        def _():
+            third_sum(0)
+            second_sum(2)
+            second_sum(3)
+            first_sum(5)
+
+        @pl.when(hp == 3)
+        def _():
+            third_sum(1)
+            last_sum(0)
+            second_sum(4)
+            start_all(pieces[7])
 
     attend_back(
         (q, 0), (k, 0), (v, 0), back_low, attn, total1,
-        (gq, 0), (gk, 0), (gv, 0), (sum_a, sum_b), True, 256, hook,
+        (gq, 0), (gk, 0), (gv, 0), (sum_a, sum_b), True, 256, self_hook,
     )
-    early(2)
-
-    def renormed(i, _):
-        here = span(i, ROWS)
-        hat, _s = normalize(x[here].astype(F32))
-        normed[here] = (hat * self_gain[...] + self_shift[...]).astype(BF)
-        return 0
-
-    lax.fori_loop(0, blocks, renormed, 0)
-    for n, ref in enumerate((gq, gk, gv)):
-        grads[:, mat(n)] = tn(normed[...], ref[...]).astype(BF)
-    late(0)
-    early(3)
+    last_sum(1)
 
     def block1(i, carry):
         here = span(i, ROWS)
@@ -867,8 +922,6 @@
     gains1 = lax.fori_loop(0, blocks, block1, (zero, zero))
     stores = [pltpu.make_async_copy(carried, grad_input_o, out_sems.at[1])]
     stores[0].start()
-    late(1)
-    early(4)
     small[...] = jnp.concatenate([*gains1, *gains2, *gains3, zero, zero], 0)
 
     def share_small(number, devices):
@@ -888,6 +941,9 @@
         return finish
 
     finish = share_small(0, [twin])
+    second_sum(5)
+    third_sum(2)
+    third_sum(3)
 
     wait_all(back_rows)
     own_rows.wait()
@@ -904,6 +960,10 @@
     lax.fori_loop(0, rows // ROWS, memory_block, 0)
     stores.append(pltpu.make_async_copy(hidden1, grad_memory_o, out_sems.at[3]))
     stores[1].start()
+    last_sum(2)
+    last_sum(3)
+    first_sum(6)
+    third_sum(4)
     fetch.wait()
     gather_all(returned, normed)
 
@@ -915,11 +975,14 @@
     lax.fori_loop(0, blocks, output_block, 0)
     stores.append(pltpu.make_async_copy(grad, layer_o, out_sems.at[4]))
     stores[2].start()
+    last_sum(4)
+    last_sum(5)
     finish()
     finish = share_small(size, [column(n) for n in range(1, layers)])
-    late(2)
-    early(5)
-    wait_all(pieces)
+    third_sum(5)
+    second_sum(6)
+    for turn in range(turns):
+        wait_all(pieces[turn])
     up_rows = up_o.shape[0]
     base = layer * piece
     for c in range(wide // width):
@@ -938,23 +1001,33 @@
     for n in range(1, layers):
         total = total + from_bias[n]
     bias_o[...] = total
-    late(3)
-    early(6)
     finish()
-    late(4)
-    late(5)
-    late(6)
+    last_sum(6)
+    third_sum(6)
+    first_sum(7)
+    second_sum(7)
+    last_sum(7)
+    third_sum(7)
     for store in stores:
         store.wait()
 
 
-def finish_kernel(reduced, project, output, query, memory, cross):
+def finish_kernel(reduced, *refs):
+    plain, (project, output, query, memory, cross), moved = refs[:5], refs[5:10], refs[10:]
     width = output.shape[1]
-    column = 0
-    for target in (project, output, query, memory, cross):
+    for pair in range(PAIRS):
+        for n in range(3):
+            column = (pair * 3 + n) * PAIR
+            project[:, n * width + pair * PAIR : n * width + (pair + 1) * PAIR] = reduced[
+                :, column : column + PAIR
+            ].astype(F32)
+    column = 3 * width
+    for target in (output, query, memory, cross):
         size = target.shape[1]
         target[...] = reduced[:, column : column + size].astype(F32)
         column += size
+    for source, target in zip(plain, moved):
+        target[...] = source[...]
 
 
 def body(
@@ -1044,7 +1117,7 @@
     back_in = [
         *big[:8], saved, hidden1, hidden2, returned_grad, rows_out, half_own, half_other,
     ]
-    count = 2 * (4 + 2 * (size - 1) + 2 * (layers - 1))
+    count = 6 * (4 + 2 * (size - 1) + 2 * (layers - 1))
     dma = pltpu.SemaphoreType.DMA
     (
         layer_output, grad_input, grad_memory, reduced, _returned, small, grad_up, grad_down, biases,
@@ -1085,6 +1158,7 @@
                 ((size - 1, by_exp, MATS * width), BF),
                 ((by_exp, MATS * width), BF),
                 ((layers - 1, by_layer, MATS * width), BF),
+                ((layers - 1, by_exp, 3 * PAIR), BF),
                 ((by_exp, MATS * width), BF),
                 ((wide, width), BF),
                 ((layers - 1, piece, width), BF),
@@ -1093,7 +1167,8 @@
             ]
         ]
         + [dma((14,)), dma((5,)), sems, sems]
-        + [dma((layers,))] * 4
+        + [dma((8 * layers,))] * 2
+        + [dma((layers,))] * 2
         + [dma((size + layers - 1,))] * 2
         + [dma((count,))] * 2,
         compiler_params=pltpu.CompilerParams(
@@ -1103,13 +1178,23 @@
     )(route, *gains, total1, total2, biases, *back_in)
     shapes = [(width, 3 * width), (width, width), (width, width), (width, 2 * width), (width, width)]
     steps = 4
-    grad_self_project, grad_self_output, grad_cross_query, grad_cross_memory, grad_cross_output = pl.pallas_call(
+    plain = [grad_input, grad_memory, layer_output, grad_up, grad_down]
+    wanted = [array(shape, F32) for shape in shapes] + [array(v.shape, v.dtype) for v in plain]
+
+    def in_steps(value):
+        return pl.BlockSpec((value.shape[0] // steps, value.shape[1]), lambda i: (i, 0))
+
+    (
+        grad_self_project, grad_self_output, grad_cross_query, grad_cross_memory, grad_cross_output,
+        grad_input, grad_memory, layer_output, grad_up, grad_down,
+    ) = pl.pallas_call(
         finish_kernel,
         grid=(steps,),
-        out_shape=tuple(array(shape, F32) for shape in shapes),
-        in_specs=[pl.BlockSpec((width // steps, MATS * width), lambda i: (i, 0))],
-        out_specs=tuple(pl.BlockSpec((width // steps, shape[1]), lambda i: (i, 0)) for shape in shapes),
-    )(reduced)
+        out_shape=tuple(wanted),
+        in_specs=[in_steps(v) for v in (reduced, *plain)],
+        out_specs=tuple(in_steps(v) for v in wanted),
+        compiler_params=pltpu.CompilerParams(vmem_limit_bytes=62 << 20),
+    )(reduced, *plain)
     index = lax.axis_index("batch")
     up_bias_sum = lax.dynamic_slice_in_dim(
         biases[: wide // width].reshape(1, wide), index * (wide // (2 * layers)), wide // (2 * layers), 1

time: 221 us -> 202 us (0.914)
  Pallas kernels: 212 us -> 199 us
  local copies, waits for them, and re-layouts: 8.07 us -> 1.78 us
    pallas_call x1, Pallas kernels: 119 us -> 102 us  [body(): pl.pallas_call(functools.partial(back_kernel, size, layers, group_rows),...]
    unnamed x21 -> x6, local copies, waits for them, and re-layouts: 6.31 us -> 0.02 us
    pallas_call x1, Pallas kernels: 5.94 us -> 9.32 us  [body(): pl.pallas_call(finish_kernel, grid=(steps,), out_shape=tuple(wanted), in_...]
where the time goes in v4:
time: 202 us; the launch traced here: 201 us
  Pallas kernels  199 us (99%)
    pallas_call x1, Pallas kernels, body(): pl.pallas_call(functools.partial(back_kernel, size, layers, group_rows),...  102 us
    pallas_call x1, Pallas kernels, body(): pl.pallas_call(functools.partial(forward_kernel, size, group_rows), out_s...  87.6 us
    pallas_call x1, Pallas kernels, body(): pl.pallas_call(finish_kernel, grid=(steps,), out_shape=tuple(wanted), in_...  9.32 us

profile of v4, /device:TPU:0, one launch (start us, length us, event | category | flops | bytes accessed | tf_op | source)
XLA Modules:
  0.0 201.3 jit_solution(16475502865000978610)
XLA Ops:
  0.7 87.6 %shard_map.322 = (bf16[10240,512]{1,0:T(8,128)(2,1)}, f32[1024,512]{1,0:T(8,128)}, f32[1024,512]{1,0:T(8,128)}, bf16[2048,512]{1,0:T(8,128)(2,1)}, bf16[2048,512...) custom-call(s32[8]{0:T(128)} %bitcast.59, ...), custom_call_target="tpu_custom_call" | custom-call | flops 60000002048 | bytes 41943040 | tf_op jit(solution)/shard_map/pallas_call | solution.py:1074
  88.2 101.9 %shard_map.323 = (bf16[1024,512]{1,0:T(8,128)(2,1)}, f32[1024,512]{1,0:T(8,128)}, f32[1024,512]{1,0:T(8,128)}, bf16[512,4096]{1,0:T(8,128)(2,1)}, bf16[2048,512]...) custom-call(s32[8]{0:T(128)} %bitcast.60, ...), custom_call_target="tpu_custom_call" | custom-call | flops 60000002048 | bytes 41943040 | tf_op jit(solution)/shard_map/pallas_call | solution.py:1124
  190.1 0.0 copy-start.1
  190.1 0.0 copy-start
  190.2 9.3 %shard_map.324 = (f32[512,1536]{1,0:T(8,128)}, f32[512,512]{1,0:T(8,128)}, f32[512,512]{1,0:T(8,128)}, f32[512,1024]{1,0:T(8,128)}, f32[512,512]{1,0:T(8,128)}, ...) custom-call(bf16[512,4096]{1,0:T(8,128)(2,1)} %get-tuple-element.56., ...), custom_call_target="tpu_custom_call" | custom-call | tf_op jit(solution)/shard_map/pallas_call | solution.py:1190
  199.5 0.0 copy-done.1
  199.5 0.6 constant_dynamic-slice_fusion.1
  200.1 0.0 copy-done
  200.1 0.6 fusion
  200.7 0.6 constant_dynamic-slice_fusion
  (3 shorter events, 0.0 us)
Async XLA Ops:
  190.1 9.3 %copy-start.1 = (f32[8,512]{1,0:T(8,128)S(1)}, f32[8,512]{1,0:T(8,128)}, u32[]{:S(2)}) copy-start(f32[8,512]{1,0:T(8,128)} %get-tuple-element.72) | copy-start | bytes 49156
  190.1 10.0 %copy-start = (f32[8,512]{1,0:T(8,128)S(1)}, f32[8,512]{1,0:T(8,128)}, u32[]{:S(2)}) copy-start(f32[8,512]{1,0:T(8,128)} %get-tuple-element.65) | copy-start | bytes 49156
